TPU v7x, 256 devices: a whole 4x4x8 slice. The times are simulated.
256 devices in a mesh: ctx: 32 (over z, x_lo, core), tp: 8 (over x_hi, y).
Axes of the slice: x: 4 (x_hi: 2, x_lo: 2; x = x_hi * 2 + x_lo), y: 4, z: 8, core: 2. Of those that a mesh axis runs over, the one named last changes fastest.
Arguments:
- layer_input: bfloat16 [16384, 5376], P('ctx', 'tp'), may hold values from -60 to 60
- norm_weight: bfloat16 [5376], P('tp'), may hold values from 0.099609375 to 1.8984375
- document_index: int32 [16384], P('ctx'), may hold values from 0 to 7, never falling along the last dimension, each value on 1 to 8192 neighbouring positions
- stored_queries: bfloat16 [16384, 4096], P('ctx', 'tp'), may hold values from -6 to 6
- stored_keys: bfloat16 [16384, 2048], P('ctx', 'tp'), may hold values from -6 to 6
- stored_values: bfloat16 [16384, 2048], P('ctx', 'tp'), may hold values from -6 to 6
- output_weight: bfloat16 [4096, 5376], P(None, 'tp'), may hold values from -0.1500248 to 0.1500248
- projection_gradient: bfloat16 [16384, 5376], P('ctx', 'tp'), may hold values from -600 to 600
- adapter_down_maps: bfloat16 [5376, 24], P('tp'), may hold values from -0.078125 to 0.078125
Outputs:
- feature_q: float32 [8, 4096], P(None, 'tp')
- feature_k: float32 [8, 2048], P(None, 'tp')
- feature_v: float32 [8, 2048], P(None, 'tp')
Inputs may be any that keep to these rules, and one draw needn't show every extreme that they name: `document_index`: document numbers never fall along the sequence; every document is one run of positions.
All inputs are finite; a program needn't handle non-finite values.
Results may differ from a plain program's by a relative error of at most 0.0095.
Values may be sent and summed in bfloat16 or wider, within the bound.
A program may use at most 128 MiB of HBM per device.

v0:
```python
import jax
import jax.numpy as jnp
from jax import lax
from jax.sharding import PartitionSpec as P

MODEL_WIDTH = 5376
QUERY_HEADS = 32
KEY_VALUE_HEADS = 16
HEAD_SIZE = 128
LOOKBACK_SPAN = 1024
ADAPTER_RANK = 8


def shifted(value, axis, steps):
    count = lax.axis_size(axis)
    first, last = (max(0, -steps), min(count, count - steps))
    return lax.ppermute(value, axis, [(source, source + steps) for source in range(first, last)])


def attend_local(query_block, key_block, value_block, gradient_block, allowed, softmax_scale):
    scores = (
        jnp.einsum("sgrd,kgd->grsk", query_block, key_block, preferred_element_type=jnp.float32)
        * softmax_scale
    )
    scores = jnp.where(allowed[None, None], scores, -1e30)
    highest = jnp.max(scores, axis=-1, keepdims=True)
    expons = jnp.exp(scores - highest)
    probs = expons / jnp.sum(expons, axis=-1, keepdims=True)
    probs_low = probs.astype(jnp.bfloat16)
    attended = jnp.einsum(
        "grsk,kgd->sgrd", probs_low, value_block, preferred_element_type=jnp.float32
    )
    delta = jnp.einsum("sgrd,sgrd->grs", gradient_block.astype(jnp.float32), attended)
    grad_probs = jnp.einsum(
        "sgrd,kgd->grsk", gradient_block, value_block, preferred_element_type=jnp.float32
    )
    grad_scores = (probs * (grad_probs - delta[..., None]) * softmax_scale).astype(jnp.bfloat16)
    query_gradient = jnp.einsum(
        "grsk,kgd->sgrd", grad_scores, key_block, preferred_element_type=jnp.float32
    )
    key_gradient = jnp.einsum(
        "grsk,sgrd->kgd", grad_scores, query_block, preferred_element_type=jnp.float32
    )
    value_gradient = jnp.einsum(
        "grsk,sgrd->kgd", probs_low, gradient_block, preferred_element_type=jnp.float32
    )
    return (query_gradient, key_gradient, value_gradient)


def per_device(
    layer_input,
    norm_weight,
    document_index,
    stored_queries,
    stored_keys,
    stored_values,
    output_weight,
    projection_gradient,
    adapter_down_maps,
):
    row_count = stored_queries.shape[0]
    hop_count = LOOKBACK_SPAN // row_count
    heads_local = stored_queries.shape[1] // HEAD_SIZE
    groups_local = stored_keys.shape[1] // HEAD_SIZE
    group_size = heads_local // groups_local
    window_rows = (hop_count + 1) * row_count
    hidden_wide = layer_input.astype(jnp.float32)
    squares_part = jnp.sum(hidden_wide * hidden_wide, axis=-1)
    mean_sq = lax.psum(squares_part, "tp") / float(MODEL_WIDTH)
    normalized_input = (
        hidden_wide * lax.rsqrt(mean_sq + 1e-06)[:, None] * norm_weight.astype(jnp.float32)[None, :]
    ).astype(jnp.bfloat16)
    reduced_part = jnp.dot(normalized_input, adapter_down_maps, preferred_element_type=jnp.float32)
    low_rows = lax.psum(reduced_part, "tp").astype(jnp.bfloat16)
    contract_cols = (((1,), (1,)), ((), ()))
    partial_value = lax.dot_general(
        projection_gradient, output_weight, contract_cols, preferred_element_type=jnp.float32
    )
    grad_full = lax.psum_scatter(partial_value, "tp", scatter_dimension=1, tiled=True)
    output_gradient = grad_full.astype(jnp.bfloat16)
    own_block = (stored_keys, stored_values, document_index.astype(jnp.bfloat16))
    earlier = []
    for distance in range(1, hop_count + 1):
        earlier.append(shifted((own_block[0], own_block[1], own_block[2]), "ctx", distance))
    ordered = earlier[::-1]
    key_all = jnp.concatenate([member[0] for member in ordered] + [stored_keys], 0)
    value_all = jnp.concatenate([member[1] for member in ordered] + [stored_values], 0)
    key_ids = jnp.concatenate(
        [member[2].astype(jnp.int32) for member in ordered] + [document_index], 0
    )
    first_row = lax.axis_index("ctx") * row_count
    query_pos = first_row + jnp.arange(row_count, dtype=jnp.int32)
    key_pos = first_row - hop_count * row_count + jnp.arange(window_rows, dtype=jnp.int32)
    spacing = query_pos[:, None] - key_pos[None, :]
    allowed = (
        (spacing >= 0)
        & (spacing < LOOKBACK_SPAN)
        & (key_pos[None, :] >= 0)
        & (document_index[:, None] == key_ids[None, :])
    )
    query_gradient, key_gradient, value_gradient = attend_local(
        stored_queries.reshape(row_count, groups_local, group_size, HEAD_SIZE),
        key_all.reshape(window_rows, groups_local, HEAD_SIZE),
        value_all.reshape(window_rows, groups_local, HEAD_SIZE),
        output_gradient.reshape(row_count, groups_local, group_size, HEAD_SIZE),
        allowed,
        float(MODEL_WIDTH // QUERY_HEADS) ** (-0.5),
    )
    query_gradient = query_gradient.reshape(row_count, heads_local * HEAD_SIZE).astype(jnp.bfloat16)
    key_terms = key_gradient.reshape(hop_count + 1, row_count, groups_local * HEAD_SIZE)
    value_terms = value_gradient.reshape(hop_count + 1, row_count, groups_local * HEAD_SIZE)
    key_sum = key_terms[hop_count]
    value_sum = value_terms[hop_count]
    for distance in range(1, hop_count + 1):
        moved = shifted(
            (key_terms[hop_count - distance], value_terms[hop_count - distance]), "ctx", -distance
        )
        key_sum = key_sum + moved[0]
        value_sum = value_sum + moved[1]
    grad_key_low = key_sum.astype(jnp.bfloat16)
    grad_value_low = value_sum.astype(jnp.bfloat16)
    contract_rows = (((0,), (0,)), ((), ()))
    adapter_query = lax.dot_general(
        low_rows[:, 0:ADAPTER_RANK],
        query_gradient,
        contract_rows,
        preferred_element_type=jnp.float32,
    )
    adapter_key = lax.dot_general(
        low_rows[:, ADAPTER_RANK : 2 * ADAPTER_RANK],
        grad_key_low,
        contract_rows,
        preferred_element_type=jnp.float32,
    )
    adapter_value = lax.dot_general(
        low_rows[:, 2 * ADAPTER_RANK : 3 * ADAPTER_RANK],
        grad_value_low,
        contract_rows,
        preferred_element_type=jnp.float32,
    )
    adapter_query, adapter_key, adapter_value = lax.psum(
        (adapter_query, adapter_key, adapter_value), "ctx"
    )
    squared_entries = (
        jnp.sum(adapter_query * adapter_query)
        + jnp.sum(adapter_key * adapter_key)
        + jnp.sum(adapter_value * adapter_value)
    )
    squared_total = lax.psum(squared_entries, "tp")
    scale_factor = jnp.sqrt(
        float(ADAPTER_RANK * (QUERY_HEADS + 2 * KEY_VALUE_HEADS) * HEAD_SIZE)
        / (squared_total + 1e-06)
    )
    return (adapter_query * scale_factor, adapter_key * scale_factor, adapter_value * scale_factor)


def solution(mesh):
    placed = (
        P("ctx", "tp"),
        P("tp"),
        P("ctx"),
        P("ctx", "tp"),
        P("ctx", "tp"),
        P("ctx", "tp"),
        P(None, "tp"),
        P("ctx", "tp"),
        P("tp", None),
    )
    return jax.shard_map(
        per_device,
        mesh=mesh,
        in_specs=placed,
        out_specs=(P(None, "tp"), P(None, "tp"), P(None, "tp")),
        check_vma=False,
    )
```

profile of v0, /device:TPU:8, one launch (start us, length us, event | category | flops | bytes accessed | tf_op | source)
XLA Modules:
  0.0 350.3 jit_solution(18138095412151333031)
XLA Ops:
  7.2 1.0 copy-done
  8.3 8.2 %fusion.37 = f32[512,4096]{1,0:T(8,128)} fusion(bf16[512,672]{0,1:T(8,128)(2,1)S(1)} %copy-done, bf16[4096,672]{0,1:T(8,128)(2,1)} %param.15), kind=kOutput, calls=%fused_computation.63 | convolution fusion | flops 2818572288 | bytes 14581760 | tf_op jit(solution)/shard_map/dot_general | solution.py:76
  16.5 0.6 copy-done.12
  17.1 1.7 collective-permute-start.3
  18.9 3.6 %collective-permute-start.2 = (bf16[512]{0:T(512)(128)(2,1)S(1)}, bf16[512]{0:T(512)(128)(2,1)S(1)}, u32[]{:S(2)}, u32[]{:S(2)}) collective-permute-start(bf16[512]{0:T(512)(128)(2,1)S(1)} %convert_element_type.50), channel_id=1, source_target_pairs={{0,16},{8,24},{16,32},{24,40},{32,48},{40,56},{48,64},{56,72},{64,... | collective-permute-start | bytes 3080 | tf_op jit(solution)/shard_map/ppermute | solution.py:17
  22.6 3.6 %collective-permute-start.5 = (bf16[512,256]{0,1:T(8,128)(2,1)S(1)}, bf16[512,256]{0,1:T(8,128)(2,1)S(1)}, u32[]{:S(2)}, u32[]{:S(2)}) collective-permute-start(bf16[512,256]{0,1:T(8,128)(2,1)S(1)} %copy.25), channel_id=1, source_target_pairs={{0,8},{8,16},{16,24},{24,32},{32,40},{40,48},{48,56},{56,64},{64,7... | collective-permute-start | bytes 786440 | tf_op jit(solution)/shard_map/ppermute | solution.py:17
  26.2 4.1 %collective-permute-start.4 = (bf16[512,256]{0,1:T(8,128)(2,1)S(1)}, bf16[512,256]{0,1:T(8,128)(2,1)}, u32[]{:S(2)}, u32[]{:S(2)}) collective-permute-start(bf16[512,256]{0,1:T(8,128)(2,1)S(1)} %copy.25), channel_id=1, source_target_pairs={{0,16},{8,24},{16,32},{24,40},{32,48},{40,56},{48,64},{56,72},{64,... | collective-permute-start | bytes 786440 | tf_op jit(solution)/shard_map/ppermute | solution.py:17
  30.5 1.9 collective-permute-start.1
  32.5 0.2 fusion.12
  32.6 25.6 %psum.42 = f32[512]{0:T(512)S(1)} all-reduce(f32[512]{0:T(512)S(1)} %fusion.12), channel_id=1, replica_groups=mesh['ctx'=32,'tp'=8] {'tp'}, use_global_device_ids=true, to_apply=%region_1.0 | all-reduce | flops 512 | bytes 4096 | tf_op jit(solution)/shard_map/psum | solution.py:69
  58.3 0.3 fusion.18
  58.5 34.7 %psum.43 = bf16[512,24]{0,1:T(8,128)(2,1)S(1)} all-reduce(f32[512,24]{0,1:T(8,128)S(1)} %fusion.18), channel_id=1, replica_groups=mesh['ctx'=32,'tp'=8] {'tp'}, use_global_device_ids=true, to_apply=%region_2.0 | all-reduce | flops 12288 | bytes 73728 | tf_op jit(solution)/shard_map/psum | solution.py:74
  93.3 0.2 copy.56
  93.5 1.5 collective-permute-start
  95.1 2.5 fusion.11
  97.6 0.7 copy-done.11
  98.3 1.1 pad_maximum_fusion.1
  99.4 5.7 %collective-permute-done = bf16[512,256]{0,1:T(8,128)(2,1)S(1)} collective-permute-done((bf16[512,256]{0,1:T(8,128)(2,1)S(1)}, bf16[512,256]{0,1:T(8,128)(2,1)S(1)}, u32[]{:S(2)}, u32[]{:S(2)}) %collective-permute-start) | collective-permute-done | bytes 262176 | tf_op jit(solution)/shard_map/ppermute | solution.py:17
  105.2 9.0 %fusion.36 = (f32[2,2,512]{2,1,0:T(2,128)S(1)}, f32[2,2,512,1536]{2,3,1,0:T(8,128)}) fusion(pred[512,1536]{0,1:T(8,128)(4,1)} %fusion.11, bf16[1536,2,128,1]{0,2,3,1:T(8,128)(2,1)S(1)} %bitcast.94, bf16[512,2,2,128]{0,3,2,1:T(8,128)(2,1)S(1)} %bitcast.98), kind=kOutput, calls=%fused_computation.62 | convolution fusion | flops 817890816 | bytes 14688256 | tf_op jit(solution)/shard_map/sub | solution.py:27
  114.2 9.1 %fusion.8 = bf16[2,2,512,1536]{2,3,1,0:T(8,128)(2,1)} fusion(f32[2,2,512,1536]{2,3,1,0:T(8,128)} %get-tuple-element.13, f32[2,2,512]{2,1,0:T(2,128)S(1)} %get-tuple-element.12), kind=kLoop, calls=%fused_computation.12 | loop fusion | flops 6291456 | bytes 18882560 | tf_op jit(solution)/shard_map/convert_element_type | solution.py:29
  123.3 4.7 %fusion.38 = f32[2,128,2,512]{3,1,2,0:T(8,128)} fusion(bf16[1536,2,128,1]{0,2,3,1:T(8,128)(2,1)S(1)} %bitcast.96, bf16[2,2,512,1536]{2,3,1,0:T(8,128)(2,1)} %fusion.8), kind=kOutput, calls=%fused_computation.64 | convolution fusion | flops 805306368 | bytes 8126464 | tf_op jit(solution)/shard_map/grsk,kgd->sgrd/dot_general | solution.py:30
  128.0 27.6 %reduce-scatter.2.cloned.1.call-done = f32[512,512]{1,0:T(8,128)} async-done(((f32[512,4096]{1,0:T(8,128)}), f32[512,512]{1,0:T(8,128)}) %reduce-scatter.2.cloned.1.call-update) | async-done | bytes 1048592 | tf_op jit(solution)/shard_map/reduce_scatter | solution.py:79
  155.7 1.3 convert_element_type.53
  157.1 1.4 copy.33
  158.5 0.4 bitcast_convert_fusion
  158.9 1.1 copy.44
  160.0 5.2 %convolution_bitcast_fusion = f32[1536,2,128]{0,2,1:T(8,128)S(1)} fusion(bf16[512,2,2,128]{0,3,2,1:T(8,128)(2,1)} %copy.33, bf16[2,2,512,1536]{2,3,1,0:T(8,128)(2,1)} %fusion.8), kind=kOutput, calls=%fused_computation.18 | convolution fusion | flops 805306368 | bytes 8388608 | tf_op jit(solution)/shard_map/grsk,sgrd->kgd/dot_general | solution.py:44
  165.2 0.9 fusion.17
  166.1 5.8 %fusion.3 = bf16[2,2,512,1536]{2,3,1,0:T(8,128)(2,1)S(1)} fusion(bf16[1536,2,128,1]{0,2,3,1:T(8,128)(2,1)S(1)} %bitcast.97, bf16[512,2,2,128]{0,3,2,1:T(8,128)(2,1)S(1)} %copy-done.6, f32[2,2,512]{2,1,0:T(2,128)S(1)} %fusion.17, f32[2,2,512,1536]{2,3,1,0:T(8,128)} %get-tuple-element.13, f32[2,2,512]{2,1,0:T(2,128)S(1)} %get-tuple-element.12), kind=kOutput, calls=%fused_computation.4 | convolution fusion | flops 821035008 | bytes 20201472 | tf_op jit(solution)/shard_map/sgrd,kgd->grsk/dot_general | solution.py:34
  172.0 2.1 convolution_bitcast_fusion.1
  174.1 0.2 fusion.35
  174.4 1.3 collective-permute-start.9
  175.7 1.3 collective-permute-start.8
  177.0 1.3 collective-permute-start.7
  178.3 1.3 collective-permute-start.6
  179.7 1.0 convolution_convert_fusion
  180.7 0.2 fusion.30
  180.9 10.3 %collective-permute-done.9 = f32[512,256]{0,1:T(8,128)S(1)} collective-permute-done((f32[512,256]{0,1:T(8,128)S(1)}, f32[512,256]{0,1:T(8,128)S(1)}, u32[]{:S(2)}, u32[]{:S(2)}) %collective-permute-start.9) | collective-permute-done | bytes 524320 | tf_op jit(solution)/shard_map/ppermute | solution.py:17
  191.2 0.2 fusion.23
  191.5 14.8 %collective-permute-done.7 = f32[512,256]{0,1:T(8,128)S(1)} collective-permute-done((f32[512,256]{0,1:T(8,128)S(1)}, f32[512,256]{0,1:T(8,128)S(1)}, u32[]{:S(2)}, u32[]{:S(2)}) %collective-permute-start.7) | collective-permute-done | bytes 524320 | tf_op jit(solution)/shard_map/ppermute | solution.py:17
  206.3 0.2 fusion.25
  206.6 109.8 %all-reduce = (f32[8,512]{1,0:T(8,128)S(1)}, f32[8,256]{1,0:T(8,128)S(1)}, f32[8,256]{1,0:T(8,128)S(1)}) all-reduce(f32[8,512]{1,0:T(8,128)S(1)} %fusion.30, f32[8,256]{1,0:T(8,128)S(1)} %fusion.28, f32[8,256]{1,0:T(8,128)S(1)} %fusion.26), channel_id=1, replica_groups=mesh['ctx'=32,'tp'=8] {'ctx'}, use_global_device_ids=true, to_apply=%region_6.7 | all-reduce | flops 8192 | bytes 65536 | tf_op jit(solution)/shard_map/psum | solution.py:141
  316.4 0.6 multiply_reduce_fusion
  317.0 0.6 multiply_reduce_fusion.1
  319.6 21.3 %psum.47 = f32[]{:T(128)} all-reduce(f32[]{:T(128)S(6)} %add.76), channel_id=1, replica_groups=mesh['ctx'=32,'tp'=8] {'tp'}, use_global_device_ids=true, to_apply=%region_12.13 | all-reduce | flops 1 | bytes 8 | tf_op jit(solution)/shard_map/psum | solution.py:149
  341.6 0.6 broadcast_multiply_fusion.1
  342.2 0.6 broadcast_multiply_fusion.2
  342.8 0.6 broadcast_multiply_fusion
  (52 shorter events, 1.1 us)
Async XLA Ops:
  7.2 1.1 copy-start
  7.2 148.5 %reduce-scatter.2.cloned.1.call-start = ((), (), s32[]{:S(2)}) async-start(), calls=%async_computation.1 | async-start | bytes 9437184 | tf_op jit(solution)/shard_map/reduce_scatter | solution.py:79
  16.4 0.7 copy-start.12
  16.4 6.0 %copy-start.9 = (bf16[512,256]{1,0:T(8,128)(2,1)S(1)}, bf16[512,256]{1,0:T(8,128)(2,1)}, u32[]{:S(2)}) copy-start(bf16[512,256]{1,0:T(8,128)(2,1)} %param.14) | copy-start | bytes 786436
  16.4 13.9 %copy-start.10 = (bf16[512,256]{1,0:T(8,128)(2,1)S(1)}, bf16[512,256]{1,0:T(8,128)(2,1)}, u32[]{:S(2)}) copy-start(bf16[512,256]{1,0:T(8,128)(2,1)} %param.13) | copy-start | bytes 786436
  16.4 16.0 %copy-start.13 = (bf16[672]{0:T(1024)(128)(2,1)S(1)}, bf16[672]{0:T(1024)(128)(2,1)}, u32[]{:S(2)}) copy-start(bf16[672]{0:T(1024)(128)(2,1)} %param.10) | copy-start | bytes 4036
  16.5 16.0 %copy-start.7 = (bf16[512,672]{0,1:T(8,128)(2,1)S(1)}, bf16[512,672]{0,1:T(8,128)(2,1)}, u32[]{:S(2)}) copy-start(bf16[512,672]{0,1:T(8,128)(2,1)} %param.9) | copy-start | bytes 2064388
  16.5 41.8 %copy-start.14 = (bf16[672,24]{0,1:T(8,128)(2,1)S(1)}, bf16[672,24]{0,1:T(8,128)(2,1)}, u32[]{:S(2)}) copy-start(bf16[672,24]{0,1:T(8,128)(2,1)} %param.17) | copy-start | bytes 96772
  16.5 76.8 %copy-start.8 = (bf16[512,512]{1,0:T(8,128)(2,1)S(1)}, bf16[512,512]{1,0:T(8,128)(2,1)}, u32[]{:S(2)}) copy-start(bf16[512,512]{1,0:T(8,128)(2,1)} %param.12) | copy-start | bytes 1572868
  17.1 76.4 %collective-permute-start.3 = (bf16[512]{0:T(512)(128)(2,1)S(1)}, bf16[512]{0:T(512)(128)(2,1)S(1)}, u32[]{:S(2)}, u32[]{:S(2)}) collective-permute-start(bf16[512]{0:T(512)(128)(2,1)S(1)} %convert_element_type.50), channel_id=1, source_target_pairs={{0,8},{8,16},{16,24},{24,32},{32,40},{40,48},{48,56},{56,64},{64,7... | collective-permute-start | bytes 3080 | tf_op jit(solution)/shard_map/ppermute | solution.py:17
  18.9 76.2 %collective-permute-start.2 = (bf16[512]{0:T(512)(128)(2,1)S(1)}, bf16[512]{0:T(512)(128)(2,1)S(1)}, u32[]{:S(2)}, u32[]{:S(2)}) collective-permute-start(bf16[512]{0:T(512)(128)(2,1)S(1)} %convert_element_type.50), channel_id=1, source_target_pairs={{0,16},{8,24},{16,32},{24,40},{32,48},{40,56},{48,64},{56,72},{64,... | collective-permute-start | bytes 3080 | tf_op jit(solution)/shard_map/ppermute | solution.py:17
  22.6 75.0 %collective-permute-start.5 = (bf16[512,256]{0,1:T(8,128)(2,1)S(1)}, bf16[512,256]{0,1:T(8,128)(2,1)S(1)}, u32[]{:S(2)}, u32[]{:S(2)}) collective-permute-start(bf16[512,256]{0,1:T(8,128)(2,1)S(1)} %copy.25), channel_id=1, source_target_pairs={{0,8},{8,16},{16,24},{24,32},{32,40},{40,48},{48,56},{56,64},{64,7... | collective-permute-start | bytes 786440 | tf_op jit(solution)/shard_map/ppermute | solution.py:17
  26.2 72.1 %collective-permute-start.4 = (bf16[512,256]{0,1:T(8,128)(2,1)S(1)}, bf16[512,256]{0,1:T(8,128)(2,1)}, u32[]{:S(2)}, u32[]{:S(2)}) collective-permute-start(bf16[512,256]{0,1:T(8,128)(2,1)S(1)} %copy.25), channel_id=1, source_target_pairs={{0,16},{8,24},{16,32},{24,40},{32,48},{40,56},{48,64},{56,72},{64,... | collective-permute-start | bytes 786440 | tf_op jit(solution)/shard_map/ppermute | solution.py:17
  30.5 68.9 %collective-permute-start.1 = (bf16[512,256]{0,1:T(8,128)(2,1)S(1)}, bf16[512,256]{0,1:T(8,128)(2,1)S(1)}, u32[]{:S(2)}, u32[]{:S(2)}) collective-permute-start(bf16[512,256]{0,1:T(8,128)(2,1)S(1)} %copy.20), channel_id=1, source_target_pairs={{0,8},{8,16},{16,24},{24,32},{32,40},{40,48},{48,56},{56,64},{64,7... | collective-permute-start | bytes 786440 | tf_op jit(solution)/shard_map/ppermute | solution.py:17
  93.5 11.6 %collective-permute-start = (bf16[512,256]{0,1:T(8,128)(2,1)S(1)}, bf16[512,256]{0,1:T(8,128)(2,1)S(1)}, u32[]{:S(2)}, u32[]{:S(2)}) collective-permute-start(bf16[512,256]{0,1:T(8,128)(2,1)S(1)} %copy.20), channel_id=1, source_target_pairs={{0,16},{8,24},{16,32},{24,40},{32,48},{40,56},{48,64},{56,72},{64,... | collective-permute-start | bytes 786440 | tf_op jit(solution)/shard_map/ppermute | solution.py:17
  97.6 0.7 copy-start.11
  99.4 23.9 %copy-start.4 = (bf16[1536,256]{0,1:T(8,128)(2,1)}, bf16[1536,256]{0,1:T(8,128)(2,1)S(1)}, u32[]{:S(2)}) copy-start(bf16[1536,256]{0,1:T(8,128)(2,1)S(1)} %pad_maximum_fusion.1) | copy-start | bytes 2359300
  105.2 9.1 %copy-start.2 = (bf16[1536,256]{0,1:T(8,128)(2,1)}, bf16[1536,256]{0,1:T(8,128)(2,1)S(1)}, u32[]{:S(2)}) copy-start(bf16[1536,256]{0,1:T(8,128)(2,1)S(1)} %pad_maximum_fusion) | copy-start | bytes 2359300
  160.0 5.3 %copy-start.1 = (f32[2,128,2,512]{3,1,2,0:T(8,128)S(1)}, f32[2,128,2,512]{3,1,2,0:T(8,128)}, u32[]{:S(2)}) copy-start(f32[2,128,2,512]{3,1,2,0:T(8,128)} %fusion.38) | copy-start | bytes 3145732
  160.0 6.1 %copy-start.5 = (bf16[1536,256]{0,1:T(8,128)(2,1)S(1)}, bf16[1536,256]{0,1:T(8,128)(2,1)}, u32[]{:S(2)}) copy-start(bf16[1536,256]{0,1:T(8,128)(2,1)} %copy-done.4) | copy-start | bytes 2359300
  160.0 6.1 %copy-start.6 = (bf16[512,2,2,128]{0,3,2,1:T(8,128)(2,1)S(1)}, bf16[512,2,2,128]{0,3,2,1:T(8,128)(2,1)}, u32[]{:S(2)}) copy-start(bf16[512,2,2,128]{0,3,2,1:T(8,128)(2,1)} %copy.33) | copy-start | bytes 1572868
  172.0 7.7 %copy-start.3 = (bf16[1536,256]{0,1:T(8,128)(2,1)S(1)}, bf16[1536,256]{0,1:T(8,128)(2,1)}, u32[]{:S(2)}) copy-start(bf16[1536,256]{0,1:T(8,128)(2,1)} %copy-done.2) | copy-start | bytes 2359300
  174.4 16.8 %collective-permute-start.9 = (f32[512,256]{0,1:T(8,128)S(1)}, f32[512,256]{0,1:T(8,128)S(1)}, u32[]{:S(2)}, u32[]{:S(2)}) collective-permute-start(f32[512,256]{0,1:T(8,128)S(1)} %bitcast.104), channel_id=1, source_target_pairs={{16,0},{24,8},{32,16},{40,24},{48,32},{56,40},{64,48},{72,56},{80,... | collective-permute-start | bytes 1572872 | tf_op jit(solution)/shard_map/ppermute | solution.py:17
  175.7 15.5 %collective-permute-start.8 = (f32[512,256]{0,1:T(8,128)S(1)}, f32[512,256]{0,1:T(8,128)S(1)}, u32[]{:S(2)}, u32[]{:S(2)}) collective-permute-start(f32[512,256]{0,1:T(8,128)S(1)} %bitcast.103), channel_id=1, source_target_pairs={{8,0},{16,8},{24,16},{32,24},{40,32},{48,40},{56,48},{64,56},{72,6... | collective-permute-start | bytes 1572872 | tf_op jit(solution)/shard_map/ppermute | solution.py:17
  177.0 29.2 %collective-permute-start.7 = (f32[512,256]{0,1:T(8,128)S(1)}, f32[512,256]{0,1:T(8,128)S(1)}, u32[]{:S(2)}, u32[]{:S(2)}) collective-permute-start(f32[512,256]{0,1:T(8,128)S(1)} %bitcast.102), channel_id=1, source_target_pairs={{16,0},{24,8},{32,16},{40,24},{48,32},{56,40},{64,48},{72,56},{80,... | collective-permute-start | bytes 1572872 | tf_op jit(solution)/shard_map/ppermute | solution.py:17
  178.3 27.9 %collective-permute-start.6 = (f32[512,256]{0,1:T(8,128)S(1)}, f32[512,256]{0,1:T(8,128)S(1)}, u32[]{:S(2)}, u32[]{:S(2)}) collective-permute-start(f32[512,256]{0,1:T(8,128)S(1)} %bitcast.101), channel_id=1, source_target_pairs={{8,0},{16,8},{24,16},{32,24},{40,32},{48,40},{56,48},{64,56},{72,6... | collective-permute-start | bytes 1572872 | tf_op jit(solution)/shard_map/ppermute | solution.py:17
Sparse Core Ops, SparseCore 0:
  16.6 138.9 reduce-scatter.1
where the time goes:
time: 354 us; the launch traced here: 350 us
  blocking collectives  191 us (54%)
  waiting for transfers between devices  58.4 us (16%)
  matrix products  36.9 us (10%)
  starting transfers between devices  21.6 us (6%)
  other arithmetic  18.9 us (5%)
  between operations  17.1 us (5%)
  local copies, waits for them, and re-layouts  5.88 us (2%)
    psum x1, blocking collectives, per_device(): lax.psum((adapter_query, adapter_key, adapter_value), 'ctx')  110 us
    psum x1, blocking collectives, per_device(): low_rows = lax.psum(reduced_part, 'tp').astype(jnp.bfloat16)  34.7 us
    ppermute x10, waiting for transfers between devices, shifted(): lax.ppermute(value, axis, [(source, source + steps) for source in range(f...  30.8 us
    reduce_scatter x1, waiting for transfers between devices, per_device(): lax.psum_scatter(partial_value, 'tp', scatter_dimension=1, tiled=True)  27.6 us
    psum x1, blocking collectives, per_device(): mean_sq = lax.psum(squares_part, 'tp') / float(MODEL_WIDTH)  25.6 us
    ppermute x10, starting transfers between devices, shifted(): lax.ppermute(value, axis, [(source, source + steps) for source in range(f...  21.6 us
    psum x1, blocking collectives, per_device(): squared_total = lax.psum(squared_entries, 'tp')  21.3 us
    convert_element_type x1, other arithmetic, attend_local(): probs_low = probs.astype(jnp.bfloat16)  9.07 us
  transfers between devices with their start and end apart: 11, of which 4 were waited for; matrix products, arithmetic and copies ran while one was open for 8% of the time, Pallas kernels for 0%

commit v1 on v0

v1 whole, which is shorter than its diff:
```python
import jax
import jax.numpy as jnp
from jax import lax
from jax.experimental import pallas as pl
from jax.experimental.pallas import tpu as pltpu
from jax.sharding import PartitionSpec as P

MODEL_WIDTH = 5376
QUERY_HEADS = 32
KEY_VALUE_HEADS = 16
HEAD_SIZE = 128
LOOKBACK_SPAN = 1024
RANK = 8

CTX = 32
ROWS = 512
WIDTH = 672
QCOLS = 512
KCOLS = 256
WINDOW = 1536
QB = 256
KSPAN = 1280
RC = 128
NRC = ROWS // RC
SCALE = float(MODEL_WIDTH // QUERY_HEADS) ** (-0.5)
LOG2E = 1.4426950408889634

MESH = pl.DeviceIdType.MESH
NT = (((1,), (1,)), ((), ()))
NN = (((1,), (0,)), ((), ()))
F32 = jnp.float32
BF16 = jnp.bfloat16


def dot(a, b, dims=NN):
    return lax.dot_general(a, b, dims, preferred_element_type=F32)


def loop(count, body):
    def step(i, carry):
        body(i)
        return carry

    lax.fori_loop(0, count, step, 0)


def kernel(
    x_ref, nw_ref, doc_ref, q_ref, k_ref, v_ref, w_ref, pg_ref, a_ref,
    oq_ref, ok_ref, ov_ref,
    xs, nws, ids, qs, kx, vx, ws, pgs, am,
    psend, pacc, precv, asend, arecv, xsend, xrecv,
    tmine, trecv, tx_send, tx_recv, lown, lx,
    bias, probs, rv, g, acc, ar, red, fin, sq, sqr,
    load_sem, wload_sem, halo_send, halo_recv,
    p_send, p_recv, a_send, a_recv, x_send, x_recv,
    t1_send, t1_recv, t2_send, t2_recv, t3_send, t3_recv, t4_send, t4_recv,
    ar_send, ar_recv, fin_send, fin_recv, sq_send, sq_recv,
):
    c = lax.axis_index("ctx")
    t = lax.axis_index("tp")
    xh = t // 4
    y = t % 4
    z = c // 4
    low = c % 4
    up = xh * 4 + (y + 1) % 4
    down = xh * 4 + (y + 3) % 4
    across = (t + 4) % 8

    def remote(src, dst, ssem, rsem, cc, tt):
        return pltpu.make_async_remote_copy(
            src_ref=src, dst_ref=dst, send_sem=ssem, recv_sem=rsem,
            device_id=(cc, tt), device_id_type=MESH,
        )

    loads = [
        pltpu.make_async_copy(src, dst, load_sem.at[n])
        for n, (src, dst) in enumerate([
            (x_ref, xs), (nw_ref, nws), (a_ref, am), (pg_ref, pgs), (q_ref, qs),
            (k_ref, kx.at[pl.ds(1024, ROWS), :]), (v_ref, vx.at[pl.ds(1024, ROWS), :]),
            (doc_ref, ids.at[:, pl.ds(1024, ROWS)]),
        ])
    ]
    for copy in loads:
        copy.start()

    def order_of(s):
        first_x = ((s + 1) // 2) % 2
        first_y = 2 + (s // 2) * ((s % 2) * 2 - 1)
        late = s - 4
        late_x = s % 2
        late_y = (1 - late // 2) * (1 + 2 * (s % 2))
        is_late = s // 4
        dx = first_x * (1 - is_late) + late_x * is_late
        dy = first_y * (1 - is_late) + late_y * is_late
        return dx * 4 + (y + dy) % 4

    def wload(s):
        rows = pl.ds(pl.multiple_of(order_of(s) * QCOLS, QCOLS), QCOLS)
        return pltpu.make_async_copy(w_ref.at[rows, :], ws.at[s], wload_sem.at[s])

    loop(8, lambda s: wload(s).start())

    barrier = pltpu.get_barrier_semaphore()

    def greet_ctx(i):
        pl.semaphore_signal(barrier, inc=1, device_id=((c + 1 + i) % CTX, t), device_id_type=MESH)

    def greet_tp(i):
        pl.semaphore_signal(barrier, inc=1, device_id=(c, (t + 1 + i) % 8), device_id_type=MESH)

    loop(CTX - 1, greet_ctx)
    loop(7, greet_tp)

    for copy in loads[:3]:
        copy.wait()
    sel_row = lax.broadcasted_iota(jnp.int32, (32, 3 * RANK), 0)
    sel_col = lax.broadcasted_iota(jnp.int32, (32, 3 * RANK), 1)
    wanted = jnp.where(sel_row < 16, sel_row + 8, jnp.where(sel_row < 24, sel_row - 16, -1))
    select = (wanted == sel_col).astype(BF16)
    maps_t = dot(select, am[...], NT).astype(BF16)
    x_wide = xs[...].astype(F32)
    xw = (x_wide * nws[...].astype(F32)).astype(BF16)
    part = dot(maps_t, xw, NT)
    square = x_wide * x_wide
    square_hi = square.astype(BF16)
    square_lo = (square - square_hi.astype(F32)).astype(BF16)
    ones = jnp.ones((RANK, WIDTH), BF16)
    squares = dot(ones, square_hi, NT) + dot(ones, square_lo, NT)
    for n in range(4):
        cols = slice(n * 128, (n + 1) * 128)
        tmine[n, 0:24, :] = part[0:24, cols]
        tmine[n, 24:32, :] = squares[:, cols]

    pl.semaphore_wait(barrier, CTX - 1 + 7)

    def t1_copy(d):
        dest = (y + d) % 4
        return remote(tmine.at[dest], trecv.at[y], t1_send.at[d], t1_recv.at[y], c, xh * 4 + dest)

    def t1_wait(d):
        src = (y + d) % 4
        remote(tmine.at[y], trecv.at[src], t1_send.at[d], t1_recv.at[src], c, t).wait_recv()
        t1_copy(d).wait_send()

    loop(3, lambda d: t1_copy(d + 1).start())

    def halo_copies(n):
        d = n + 1
        dest = (c + d) % CTX
        rows = pl.ds((2 - d) * ROWS, ROWS)
        return [
            remote(k_ref, kx.at[rows, :], halo_send.at[n, 0], halo_recv.at[n, 0], dest, t),
            remote(doc_ref, ids.at[:, rows], halo_send.at[n, 1], halo_recv.at[n, 1], dest, t),
            remote(v_ref, vx.at[rows, :], halo_send.at[n, 2], halo_recv.at[n, 2], dest, t),
        ]

    halos = [halo_copies(0), halo_copies(1)]
    for m in range(3):
        for n in range(2):
            halos[n][m].start()

    loads[3].wait()

    def rows_of(rc):
        return pl.ds(pl.multiple_of(rc * RC, RC), RC)

    def p_copy(s, rc):
        turn = (y + 1 + 2 * (s % 2)) % 4
        return remote(
            psend.at[s, rows_of(rc), :], precv.at[s, rows_of(rc), :],
            p_send.at[s, rc], p_recv.at[s, rc], c, xh * 4 + turn,
        )

    def early(s):
        wload(s).wait()
        psend[s] = dot(pgs[...], ws[s], NT).astype(BF16)
        loop(NRC, lambda rc: p_copy(s, rc).start())

    loop(4, early)

    loop(3, lambda d: t1_wait(d + 1))
    tsum = tmine[y]
    for d in range(1, 4):
        tsum = tsum + trecv[(y + d) % 4]
    tx_send[...] = tsum
    t2 = remote(tx_send, tx_recv, t2_send, t2_recv, c, across)
    t2.start()

    def late(s):
        wload(s + 4).wait()
        pacc[s] = dot(pgs[...], ws[s + 4], NT)

    loop(4, late)

    t2.wait()
    tfull = tx_send[...] + tx_recv[...]
    rstd = lax.rsqrt(tfull[24:32, :] * (1.0 / MODEL_WIDTH) + 1e-06)
    lown[...] = (tfull * jnp.concatenate([rstd] * 4, axis=0)).astype(BF16)

    def own_cols(n):
        return pl.ds(pl.multiple_of(1024 + n * 128, 128), 128)

    lx[:, own_cols(y)] = lown[...]

    def t3_copy(d):
        return remote(
            lown, lx.at[:, own_cols(y)], t3_send.at[d], t3_recv.at[y], c, xh * 4 + (y + d) % 4
        )

    def t3_wait(d):
        src = (y + d) % 4
        remote(lown, lx.at[:, own_cols(src)], t3_send.at[d], t3_recv.at[src], c, t).wait_recv()
        t3_copy(d).wait_send()

    loop(3, lambda d: t3_copy(d + 1).start())

    def a_copy(s, rc):
        turn = (y + 1 + 2 * s) % 4
        return remote(
            asend.at[s, rows_of(rc), :], arecv.at[s, rows_of(rc), :],
            a_send.at[s, rc], a_recv.at[s, rc], c, xh * 4 + turn,
        )

    def pass_on(i):
        rc, s = i // 2, i % 2
        p_copy(s, rc).wait_recv()
        asend[s, rows_of(rc), :] = (
            pacc[s, rows_of(rc), :] + precv[s, rows_of(rc), :].astype(F32)
        ).astype(BF16)
        a_copy(s, rc).start()

    loop(2 * NRC, pass_on)

    loop(3, lambda d: t3_wait(d + 1))
    t4s = [
        remote(
            lx.at[pl.ds(0, 16), pl.ds(1024, ROWS)], lx.at[pl.ds(0, 16), pl.ds((1 - n) * ROWS, ROWS)],
            t4_send.at[n], t4_recv.at[n], (c + n + 1) % CTX, t,
        )
        for n in range(2)
    ]
    for copy in t4s:
        copy.start()

    for copy in loads[4:]:
        copy.wait()
    for n in range(2):
        halos[n][0].wait()
        halos[n][1].wait()
    key_at = lax.broadcasted_iota(jnp.int32, (1, WINDOW), 1) + c * ROWS - LOOKBACK_SPAN
    key_ids = jnp.where(key_at < 0, -1, ids[...]).astype(F32)
    own_ids = jnp.broadcast_to(key_ids[:, 1024:1536], (128, ROWS))
    query_ids = jnp.transpose(own_ids, (1, 0))
    row_at = lax.broadcasted_iota(jnp.int32, (QB, 128), 0)
    col_at = lax.broadcasted_iota(jnp.int32, (QB, 128), 1)
    for b in range(2):
        for m in range(KSPAN // 128):
            spacing = 1024 - m * 128 + row_at - col_at
            start = b * QB + m * 128
            allowed = (
                (spacing >= 0)
                & (spacing < LOOKBACK_SPAN)
                & (query_ids[b * QB:(b + 1) * QB, :] == key_ids[:, start:start + 128])
            )
            bias[b, :, m * 128:(m + 1) * 128] = jnp.where(allowed, 0.0, -1e30)

    def parts_of(i):
        h, b = i // 2, i % 2
        q_rows = pl.ds(pl.multiple_of(b * QB, QB), QB)
        k_rows = pl.ds(pl.multiple_of(b * QB, QB), KSPAN)
        h_cols = pl.ds(pl.multiple_of(h * HEAD_SIZE, HEAD_SIZE), HEAD_SIZE)
        g_cols = pl.ds(pl.multiple_of((h // 2) * HEAD_SIZE, HEAD_SIZE), HEAD_SIZE)
        return h, b, q_rows, k_rows, h_cols, g_cols

    def softmax(i):
        h, b, q_rows, k_rows, h_cols, g_cols = parts_of(i)
        scores = dot(qs[q_rows, h_cols], kx[k_rows, g_cols], NT) * (SCALE * LOG2E) + bias[b]
        highest = jnp.max(scores, axis=-1, keepdims=True)
        expons = jnp.exp2(scores - highest)
        total = jnp.sum(expons, axis=-1, keepdims=True)
        probs[i] = expons * (1.0 / total)

    loop(8, softmax)

    for copy in t4s:
        copy.wait()

    def value_side(i):
        b = i % 2
        lows = lx[0:16, pl.ds(pl.multiple_of(b * QB, QB), KSPAN)]
        rv[i] = dot(lows, probs[i].astype(BF16), NT)

    loop(8, value_side)

    def x_copy(rc):
        return remote(
            xsend.at[rows_of(rc), :], xrecv.at[rows_of(rc), :],
            x_send.at[rc], x_recv.at[rc], c, across,
        )

    def finish(rc):
        rows = rows_of(rc)
        p_copy(2, rc).wait_recv()
        p_copy(3, rc).wait_recv()
        a_copy(0, rc).wait_recv()
        a_copy(1, rc).wait_recv()
        xsend[rows, :] = (
            pacc[3 - xh, rows, :] + arecv[1 - xh, rows, :].astype(F32)
            + precv[2 + xh, rows, :].astype(F32)
        ).astype(BF16)
        x_copy(rc).start()
        pacc[2 + xh, rows, :] = (
            pacc[2 + xh, rows, :] + arecv[xh, rows, :].astype(F32)
            + precv[3 - xh, rows, :].astype(F32)
        )

    loop(NRC, finish)

    for n in range(2):
        halos[n][2].wait()
    acc[...] = jnp.zeros_like(acc)

    def take(rc):
        rows = rows_of(rc)
        x_copy(rc).wait_recv()
        g[rows, :] = (pacc[2 + xh, rows, :] + xrecv[rows, :].astype(F32)).astype(BF16)

    def backward(b, h):
        i = h * 2 + b
        h, b, q_rows, k_rows, h_cols, g_cols = parts_of(i)
        grad = g[q_rows, h_cols]
        keys = kx[k_rows, g_cols]
        grad_probs = dot(grad, vx[k_rows, g_cols], NT)
        prob = probs[i]
        delta = jnp.sum(prob * grad_probs, axis=-1, keepdims=True)
        grad_scores = (prob * (grad_probs - delta)).astype(BF16)
        lows = lx[0:16, k_rows]
        side_k = (dot(lows, grad_scores, NT) * SCALE).astype(BF16)
        own = lx[16:32, pl.ds(pl.multiple_of(1024 + b * QB, QB), QB)]
        side_q = (dot(own, grad_scores) * SCALE).astype(BF16)
        acc[h] += dot(side_q, keys)[0:8]
        acc[4 + h // 2] += dot(side_k, qs[q_rows, h_cols])[0:8]
        acc[6 + h // 2] += dot(rv[i].astype(BF16), grad)[8:16]

    def block(b):
        loop(2, lambda n: take(b * 2 + n))
        loop(4, lambda h: backward(b, h))

    loop(2, block)

    def ar_copy(d):
        dest = (c + d) % CTX
        return remote(acc.at[dest // 4], ar.at[c], ar_send.at[d], ar_recv.at[c], dest, t)

    def ar_wait(d):
        src = (c + d) % CTX
        remote(acc.at[z], ar.at[src], ar_send.at[d], ar_recv.at[src], c, t).wait_recv()

    loop(CTX - 1, lambda d: ar_copy(d + 1).start())
    ar[c] = acc[z]
    loop(CTX - 1, lambda d: ar_wait(d + 1))
    red[...] = jnp.sum(ar[...], axis=0)

    def fin_copy(d):
        return remote(
            red, fin.at[z], fin_send.at[d], fin_recv.at[z], ((z + d) % 8) * 4 + low, t
        )

    def fin_wait(d):
        src = (z + d) % 8
        remote(red, fin.at[src], fin_send.at[d], fin_recv.at[src], c, t).wait_recv()

    loop(7, lambda d: fin_copy(d + 1).start())
    fin[z] = red[...]
    loop(7, lambda d: fin_wait(d + 1))

    whole = fin[...]
    sq[...] = jnp.sum(whole * whole, axis=0)

    def sq_copy(d):
        return remote(sq, sqr.at[t], sq_send.at[d], sq_recv.at[t], c, (t + d) % 8)

    def sq_wait(d):
        src = (t + d) % 8
        remote(sq, sqr.at[src], sq_send.at[d], sq_recv.at[src], c, t).wait_recv()

    loop(7, lambda d: sq_copy(d + 1).start())
    sqr[t] = sq[...]
    loop(7, lambda d: sq_wait(d + 1))
    squared = jnp.sum(jnp.sum(jnp.sum(sqr[...], axis=0), axis=0, keepdims=True), axis=1, keepdims=True)
    factor = jnp.sqrt(
        float(RANK * (QUERY_HEADS + 2 * KEY_VALUE_HEADS) * HEAD_SIZE) / (squared + 1e-06)
    )
    for n in range(4):
        oq_ref[:, n * 128:(n + 1) * 128] = fin[n] * factor
    for n in range(2):
        ok_ref[:, n * 128:(n + 1) * 128] = fin[4 + n] * factor
        ov_ref[:, n * 128:(n + 1) * 128] = fin[6 + n] * factor

    def drain(i):
        p_copy(i // NRC, i % NRC).wait_send()

    loop(4 * NRC, drain)
    loop(2 * NRC, lambda i: a_copy(i // NRC, i % NRC).wait_send())
    loop(NRC, lambda rc: x_copy(rc).wait_send())
    loop(CTX - 1, lambda d: ar_copy(d + 1).wait_send())
    loop(7, lambda d: fin_copy(d + 1).wait_send())
    loop(7, lambda d: sq_copy(d + 1).wait_send())


def per_device(x, nw, doc, q, k, v, w, pg, a):
    any_spec = pl.BlockSpec(memory_space=pl.ANY)
    vmem = pl.BlockSpec(memory_space=pltpu.VMEM)
    dma = pltpu.SemaphoreType.DMA
    return pl.pallas_call(
        kernel,
        out_shape=(
            jax.ShapeDtypeStruct((RANK, QCOLS), F32),
            jax.ShapeDtypeStruct((RANK, KCOLS), F32),
            jax.ShapeDtypeStruct((RANK, KCOLS), F32),
        ),
        in_specs=[any_spec] * 9,
        out_specs=(vmem, vmem, vmem),
        scratch_shapes=[
            pltpu.VMEM((ROWS, WIDTH), BF16),
            pltpu.VMEM((1, WIDTH), BF16),
            pltpu.VMEM((1, WINDOW), jnp.int32),
            pltpu.VMEM((ROWS, QCOLS), BF16),
            pltpu.VMEM((WINDOW, KCOLS), BF16),
            pltpu.VMEM((WINDOW, KCOLS), BF16),
            pltpu.VMEM((8, QCOLS, WIDTH), BF16),
            pltpu.VMEM((ROWS, WIDTH), BF16),
            pltpu.VMEM((WIDTH, 3 * RANK), BF16),
            pltpu.VMEM((4, ROWS, QCOLS), BF16),
            pltpu.VMEM((4, ROWS, QCOLS), F32),
            pltpu.VMEM((4, ROWS, QCOLS), BF16),
            pltpu.VMEM((2, ROWS, QCOLS), BF16),
            pltpu.VMEM((2, ROWS, QCOLS), BF16),
            pltpu.VMEM((ROWS, QCOLS), BF16),
            pltpu.VMEM((ROWS, QCOLS), BF16),
            pltpu.VMEM((4, 32, 128), F32),
            pltpu.VMEM((4, 32, 128), F32),
            pltpu.VMEM((32, 128), F32),
            pltpu.VMEM((32, 128), F32),
            pltpu.VMEM((32, 128), BF16),
            pltpu.VMEM((32, WINDOW), BF16),
            pltpu.VMEM((2, QB, KSPAN), F32),
            pltpu.VMEM((8, QB, KSPAN), F32),
            pltpu.VMEM((8, 16, QB), F32),
            pltpu.VMEM((ROWS, QCOLS), BF16),
            pltpu.VMEM((8, RANK, 128), F32),
            pltpu.VMEM((CTX, RANK, 128), F32),
            pltpu.VMEM((RANK, 128), F32),
            pltpu.VMEM((8, RANK, 128), F32),
            pltpu.VMEM((RANK, 128), F32),
            pltpu.VMEM((8, RANK, 128), F32),
            dma((8,)), dma((8,)), dma((2, 3)), dma((2, 3)),
            dma((4, NRC)), dma((4, NRC)), dma((2, NRC)), dma((2, NRC)), dma((NRC,)), dma((NRC,)),
            dma((4,)), dma((4,)), dma, dma, dma((4,)), dma((4,)), dma((2,)), dma((2,)),
            dma((CTX,)), dma((CTX,)), dma((8,)), dma((8,)), dma((8,)), dma((8,)),
        ],
        compiler_params=pltpu.CompilerParams(
            collective_id=0, has_side_effects=True, vmem_limit_bytes=60 * 1024 * 1024
        ),
        cost_estimate=pl.CostEstimate(
            flops=8_000_000_000, bytes_accessed=10_000_000, transcendentals=3_000_000
        ),
    )(x, nw.reshape(1, WIDTH), doc.reshape(1, ROWS), q, k, v, w, pg, a)


def solution(mesh):
    placed = (
        P("ctx", "tp"),
        P("tp"),
        P("ctx"),
        P("ctx", "tp"),
        P("ctx", "tp"),
        P("ctx", "tp"),
        P(None, "tp"),
        P("ctx", "tp"),
        P("tp", None),
    )
    return jax.shard_map(
        per_device,
        mesh=mesh,
        in_specs=placed,
        out_specs=(P(None, "tp"), P(None, "tp"), P(None, "tp")),
        check_vma=False,
    )
```

time: 354 us -> 102 us (0.29)
  blocking collectives: 191 us -> 0 us
  Pallas kernels: 0 us -> 80 us
  waiting for transfers between devices: 58.4 us -> 0 us
  matrix products: 36.9 us -> 0 us
  starting transfers between devices: 21.6 us -> 0 us
  other arithmetic: 18.9 us -> 0 us
  between operations: 17.1 us -> 0.64 us
  local copies, waits for them, and re-layouts: 5.88 us -> 19.6 us
    psum x4 -> x0, blocking collectives: 191 us -> none  [the longest x1 110 us: per_device(): lax.psum((adapter_query, adapter_key, adapter_value), 'ctx')]
    pallas_call x0 -> x1, Pallas kernels: none -> 80 us  [per_device(): pl.pallas_call(kernel, out_shape=(jax.ShapeDtypeStruct((RANK, QCOLS), F32...]
    ppermute x10 -> x0, waiting for transfers between devices: 30.8 us -> none  [shifted(): lax.ppermute(value, axis, [(source, source + steps) for source in range(f...]
    dot_general x10 -> x0, matrix products: 27.9 us -> none  [the longest x1 8.17 us: per_device(): lax.dot_general(projection_gradient, output_weight, contract_cols, prefer...]
    reduce_scatter x1 -> x0, waiting for transfers between devices: 27.6 us -> none  [per_device(): lax.psum_scatter(partial_value, 'tp', scatter_dimension=1, tiled=True)]
    ppermute x10 -> x0, starting transfers between devices: 21.6 us -> none  [shifted(): lax.ppermute(value, axis, [(source, source + steps) for source in range(f...]
    unnamed x33 -> x7, local copies, waits for them, and re-layouts: 3.78 us -> 18.3 us
    convert_element_type x8 -> x0, other arithmetic: 10.7 us -> none  [the longest x1 9.07 us: attend_local(): probs_low = probs.astype(jnp.bfloat16)]
  transfers between devices with their start and end apart: 11 -> 0, of which waited for: 4 -> 0; matrix products, arithmetic and copies ran while one was open for 8% -> 0% of each run, Pallas kernels for 0% -> 0%
where the time goes in v1:
time: 102 us; the launch traced here: 100 us
  Pallas kernels  80 us (78%)
  local copies, waits for them, and re-layouts  19.6 us (19%)
    pallas_call x1, Pallas kernels, per_device(): pl.pallas_call(kernel, out_shape=(jax.ShapeDtypeStruct((RANK, QCOLS), F32...  80 us
    unnamed x7, local copies, waits for them, and re-layouts  18.3 us

profile of v1, /device:TPU:8, one launch (start us, length us, event | category | flops | bytes accessed | tf_op | source)
XLA Modules:
  0.0 100.2 jit_solution(13243814848677691781)
XLA Ops:
  0.6 1.3 %reshape.12.nw_ref = bf16[1,672]{1,0:T(2,128)(2,1)} reshape(bf16[672]{0:T(1024)(128)(2,1)} %param.10) | data formatting | bytes 2688 | tf_op jit(solution)/shard_map/reshape | solution.py:468
  1.9 1.6 %copy.15.a_ref = bf16[672,24]{1,0:T(8,128)(2,1)} copy(bf16[672,24]{0,1:T(8,128)(2,1)} %param.17) | data formatting | bytes 64512 | tf_op args[8]
  3.5 2.3 %copy.12.x_ref = bf16[512,672]{1,0:T(8,128)(2,1)} copy(bf16[512,672]{0,1:T(8,128)(2,1)} %param.9) | data formatting | bytes 1376256 | tf_op args[0]
  5.7 2.3 %copy.14.pg_ref = bf16[512,672]{1,0:T(8,128)(2,1)} copy(bf16[512,672]{0,1:T(8,128)(2,1)} %param.16) | data formatting | bytes 1376256 | tf_op args[7]
  8.0 8.3 %copy.13.w_ref = bf16[4096,672]{1,0:T(8,128)(2,1)} copy(bf16[4096,672]{0,1:T(8,128)(2,1)} %param.15) | data formatting | bytes 11010048 | tf_op args[6]
  16.3 80.0 %shard_map.112 = (f32[8,512]{1,0:T(8,128)}, f32[8,256]{1,0:T(8,128)}, f32[8,256]{1,0:T(8,128)}) custom-call(bf16[512,672]{1,0:T(8,128)(2,1)} %copy.12.x_ref, bf16[1,672]{1,0:T(2,128)(2,1)} %reshape.12.nw_ref, s32[1,512]{1,0:T(1,128)} %bitcast.1, bf16[512,512]{1,0:T(8,128)(2,1)} %q_ref.1, bf16[512,256]{1,0:T(8,128)(2,1)} %k_ref.1, bf16[512,256]{1,0:T(8,128)(2,1)} %v_ref.1, ...), custom_call_target="tpu_custom_call" | custom-call | flops 8000000000 | bytes 10000000 | tf_op jit(solution)/shard_map/pallas_call | solution.py:415
  96.3 1.3 %copy.19 = f32[8,512]{1,0:T(8,128)} copy(f32[8,512]{1,0:T(8,128)} %get-tuple-element.6) | data formatting | bytes 32768
  97.6 1.3 %copy.20 = f32[8,256]{1,0:T(8,128)} copy(f32[8,256]{1,0:T(8,128)} %get-tuple-element.7) | data formatting | bytes 16384
  98.9 1.3 %copy.21 = f32[8,256]{1,0:T(8,128)} copy(f32[8,256]{1,0:T(8,128)} %get-tuple-element.8) | data formatting | bytes 16384

commit v2 on v1

--- a/solution.py
+++ b/solution.py
@@ -46,8 +46,8 @@
 
 def kernel(
     x_ref, nw_ref, doc_ref, q_ref, k_ref, v_ref, w_ref, pg_ref, a_ref,
-    oq_ref, ok_ref, ov_ref,
-    xs, nws, ids, qs, kx, vx, ws, pgs, am,
+    out_ref,
+    xs, nws, ids, qs, kx, vx, ws, pgt, pgs, am,
     psend, pacc, precv, asend, arecv, xsend, xrecv,
     tmine, trecv, tx_send, tx_recv, lown, lx,
     bias, probs, rv, g, acc, ar, red, fin, sq, sqr,
@@ -75,7 +75,7 @@
     loads = [
         pltpu.make_async_copy(src, dst, load_sem.at[n])
         for n, (src, dst) in enumerate([
-            (x_ref, xs), (nw_ref, nws), (a_ref, am), (pg_ref, pgs), (q_ref, qs),
+            (x_ref, xs), (nw_ref, nws), (a_ref, am), (pg_ref, pgt), (q_ref, qs),
             (k_ref, kx.at[pl.ds(1024, ROWS), :]), (v_ref, vx.at[pl.ds(1024, ROWS), :]),
             (doc_ref, ids.at[:, pl.ds(1024, ROWS)]),
         ])
@@ -95,8 +95,8 @@
         return dx * 4 + (y + dy) % 4
 
     def wload(s):
-        rows = pl.ds(pl.multiple_of(order_of(s) * QCOLS, QCOLS), QCOLS)
-        return pltpu.make_async_copy(w_ref.at[rows, :], ws.at[s], wload_sem.at[s])
+        cols = pl.ds(pl.multiple_of(order_of(s) * QCOLS, QCOLS), QCOLS)
+        return pltpu.make_async_copy(w_ref.at[:, cols], ws.at[s], wload_sem.at[s])
 
     loop(8, lambda s: wload(s).start())
 
@@ -117,19 +117,43 @@
     sel_col = lax.broadcasted_iota(jnp.int32, (32, 3 * RANK), 1)
     wanted = jnp.where(sel_row < 16, sel_row + 8, jnp.where(sel_row < 24, sel_row - 16, -1))
     select = (wanted == sel_col).astype(BF16)
-    maps_t = dot(select, am[...], NT).astype(BF16)
-    x_wide = xs[...].astype(F32)
-    xw = (x_wide * nws[...].astype(F32)).astype(BF16)
-    part = dot(maps_t, xw, NT)
+    maps = dot(select, am[...]) * nws[...].astype(F32).reshape(1, WIDTH)
+    maps_hi = maps.astype(BF16)
+    maps_lo = (maps - maps_hi.astype(F32)).astype(BF16)
+    x_low = xs[...]
+    part = dot(maps_hi, x_low) + dot(maps_lo, x_low)
+    x_wide = x_low.astype(F32)
     square = x_wide * x_wide
     square_hi = square.astype(BF16)
     square_lo = (square - square_hi.astype(F32)).astype(BF16)
     ones = jnp.ones((RANK, WIDTH), BF16)
-    squares = dot(ones, square_hi, NT) + dot(ones, square_lo, NT)
+    squares = dot(ones, square_hi) + dot(ones, square_lo)
     for n in range(4):
         cols = slice(n * 128, (n + 1) * 128)
         tmine[n, 0:24, :] = part[0:24, cols]
         tmine[n, 24:32, :] = squares[:, cols]
+
+    def rows_of(rc):
+        return pl.ds(pl.multiple_of(rc * RC, RC), RC)
+
+    def p_copy(s, rc):
+        turn = (y + 1 + 2 * (s % 2)) % 4
+        return remote(
+            psend.at[s, rows_of(rc), :], precv.at[s, rows_of(rc), :],
+            p_send.at[s, rc], p_recv.at[s, rc], c, xh * 4 + turn,
+        )
+
+    def early(s):
+        wload(s).wait()
+        psend[s] = dot(pgs[...], ws[s]).astype(BF16)
+
+    def late(s):
+        wload(s + 4).wait()
+        pacc[s] = dot(pgs[...], ws[s + 4])
+
+    loads[3].wait()
+    pgs[...] = jnp.transpose(pgt[...], (1, 0))
+    loop(2, early)
 
     pl.semaphore_wait(barrier, CTX - 1 + 7)
 
@@ -155,28 +179,23 @@
         ]
 
     halos = [halo_copies(0), halo_copies(1)]
-    for m in range(3):
+    for n in range(2):
+        p_copy(n, 0).start()
+    for m in range(2):
         for n in range(2):
             halos[n][m].start()
-
-    loads[3].wait()
-
-    def rows_of(rc):
-        return pl.ds(pl.multiple_of(rc * RC, RC), RC)
-
-    def p_copy(s, rc):
-        turn = (y + 1 + 2 * (s % 2)) % 4
-        return remote(
-            psend.at[s, rows_of(rc), :], precv.at[s, rows_of(rc), :],
-            p_send.at[s, rc], p_recv.at[s, rc], c, xh * 4 + turn,
-        )
-
-    def early(s):
-        wload(s).wait()
-        psend[s] = dot(pgs[...], ws[s], NT).astype(BF16)
-        loop(NRC, lambda rc: p_copy(s, rc).start())
-
-    loop(4, early)
+    for n in range(2):
+        p_copy(n, 1).start()
+
+    def p_next(s, rc, s_before, rc_before):
+        for n in range(2):
+            p_copy(s_before + n, rc_before).wait_send()
+            p_copy(s + n, rc).start()
+
+    loop(2, lambda s: early(s + 2))
+    p_next(0, 2, 0, 0)
+    for n in range(2):
+        halos[n][2].start()
 
     loop(3, lambda d: t1_wait(d + 1))
     tsum = tmine[y]
@@ -186,11 +205,10 @@
     t2 = remote(tx_send, tx_recv, t2_send, t2_recv, c, across)
     t2.start()
 
-    def late(s):
-        wload(s + 4).wait()
-        pacc[s] = dot(pgs[...], ws[s + 4], NT)
-
-    loop(4, late)
+    loop(2, late)
+    p_next(0, 3, 0, 1)
+    loop(2, lambda s: late(s + 2))
+    p_next(2, 0, 0, 2)
 
     t2.wait()
     tfull = tx_send[...] + tx_recv[...]
@@ -221,15 +239,17 @@
             a_send.at[s, rc], a_recv.at[s, rc], c, xh * 4 + turn,
         )
 
-    def pass_on(i):
-        rc, s = i // 2, i % 2
-        p_copy(s, rc).wait_recv()
-        asend[s, rows_of(rc), :] = (
-            pacc[s, rows_of(rc), :] + precv[s, rows_of(rc), :].astype(F32)
-        ).astype(BF16)
-        a_copy(s, rc).start()
-
-    loop(2 * NRC, pass_on)
+    def pass_on(rc):
+        for n in range(2):
+            p_copy(n, rc).wait_recv()
+            asend[n, rows_of(rc), :] = (
+                pacc[n, rows_of(rc), :] + precv[n, rows_of(rc), :].astype(F32)
+            ).astype(BF16)
+
+    pass_on(0)
+    for n in range(2):
+        p_copy(n, 3).wait_send()
+        a_copy(n, 0).start()
 
     loop(3, lambda d: t3_wait(d + 1))
     t4s = [
@@ -280,17 +300,10 @@
         total = jnp.sum(expons, axis=-1, keepdims=True)
         probs[i] = expons * (1.0 / total)
 
-    loop(8, softmax)
-
-    for copy in t4s:
-        copy.wait()
-
     def value_side(i):
         b = i % 2
         lows = lx[0:16, pl.ds(pl.multiple_of(b * QB, QB), KSPAN)]
         rv[i] = dot(lows, probs[i].astype(BF16), NT)
-
-    loop(8, value_side)
 
     def x_copy(rc):
         return remote(
@@ -313,12 +326,6 @@
             pacc[2 + xh, rows, :] + arecv[xh, rows, :].astype(F32)
             + precv[3 - xh, rows, :].astype(F32)
         )
-
-    loop(NRC, finish)
-
-    for n in range(2):
-        halos[n][2].wait()
-    acc[...] = jnp.zeros_like(acc)
 
     def take(rc):
         rows = rows_of(rc)
@@ -342,11 +349,44 @@
         acc[4 + h // 2] += dot(side_k, qs[q_rows, h_cols])[0:8]
         acc[6 + h // 2] += dot(rv[i].astype(BF16), grad)[8:16]
 
-    def block(b):
-        loop(2, lambda n: take(b * 2 + n))
-        loop(4, lambda h: backward(b, h))
-
-    loop(2, block)
+    acc[...] = jnp.zeros_like(acc)
+    for n in range(2):
+        p_copy(2 + n, 0).wait_send()
+        p_copy(2 + n, 1).start()
+    loop(3, softmax)
+    pass_on(1)
+    for n in range(2):
+        a_copy(n, 1).start()
+    loop(3, lambda i: softmax(i + 3))
+    for n in range(2):
+        a_copy(n, 0).wait_send()
+        p_copy(2 + n, 2).start()
+    loop(2, lambda i: softmax(i + 6))
+    finish(0)
+    pass_on(2)
+    for n in range(2):
+        p_copy(2 + n, 1).wait_send()
+        a_copy(n, 2).start()
+    for copy in t4s:
+        copy.wait()
+    loop(4, value_side)
+    finish(1)
+    for n in range(2):
+        a_copy(n, 1).wait_send()
+        p_copy(2 + n, 3).start()
+    loop(4, lambda i: value_side(i + 4))
+    pass_on(3)
+    for n in range(2):
+        p_copy(2 + n, 2).wait_send()
+        a_copy(n, 3).start()
+    for n in range(2):
+        halos[n][2].wait()
+    loop(2, take)
+    loop(4, lambda h: backward(0, h))
+    finish(2)
+    finish(3)
+    loop(2, lambda n: take(n + 2))
+    loop(4, lambda h: backward(1, h))
 
     def ar_copy(d):
         dest = (c + d) % CTX
@@ -356,7 +396,7 @@
         src = (c + d) % CTX
         remote(acc.at[z], ar.at[src], ar_send.at[d], ar_recv.at[src], c, t).wait_recv()
 
-    loop(CTX - 1, lambda d: ar_copy(d + 1).start())
+    loop(CTX - 1, lambda i: ar_copy(16 + (i + 1) // 2 * (2 * (i % 2) - 1)).start())
     ar[c] = acc[z]
     loop(CTX - 1, lambda d: ar_wait(d + 1))
     red[...] = jnp.sum(ar[...], axis=0)
@@ -370,7 +410,7 @@
         src = (z + d) % 8
         remote(red, fin.at[src], fin_send.at[d], fin_recv.at[src], c, t).wait_recv()
 
-    loop(7, lambda d: fin_copy(d + 1).start())
+    loop(7, lambda i: fin_copy(4 + (i + 1) // 2 * (2 * (i % 2) - 1)).start())
     fin[z] = red[...]
     loop(7, lambda d: fin_wait(d + 1))
 
@@ -391,46 +431,46 @@
     factor = jnp.sqrt(
         float(RANK * (QUERY_HEADS + 2 * KEY_VALUE_HEADS) * HEAD_SIZE) / (squared + 1e-06)
     )
-    for n in range(4):
-        oq_ref[:, n * 128:(n + 1) * 128] = fin[n] * factor
-    for n in range(2):
-        ok_ref[:, n * 128:(n + 1) * 128] = fin[4 + n] * factor
-        ov_ref[:, n * 128:(n + 1) * 128] = fin[6 + n] * factor
-
-    def drain(i):
-        p_copy(i // NRC, i % NRC).wait_send()
-
-    loop(4 * NRC, drain)
-    loop(2 * NRC, lambda i: a_copy(i // NRC, i % NRC).wait_send())
+    out_ref[...] = fin[...] * factor
+
+    for n in range(2):
+        p_copy(2 + n, 3).wait_send()
+        a_copy(n, 2).wait_send()
+        a_copy(n, 3).wait_send()
     loop(NRC, lambda rc: x_copy(rc).wait_send())
     loop(CTX - 1, lambda d: ar_copy(d + 1).wait_send())
     loop(7, lambda d: fin_copy(d + 1).wait_send())
     loop(7, lambda d: sq_copy(d + 1).wait_send())
 
 
+def split(sum_ref, oq_ref, ok_ref, ov_ref):
+    for n in range(4):
+        oq_ref[:, n * 128:(n + 1) * 128] = sum_ref[n]
+    for n in range(2):
+        ok_ref[:, n * 128:(n + 1) * 128] = sum_ref[4 + n]
+        ov_ref[:, n * 128:(n + 1) * 128] = sum_ref[6 + n]
+
+
 def per_device(x, nw, doc, q, k, v, w, pg, a):
     any_spec = pl.BlockSpec(memory_space=pl.ANY)
     vmem = pl.BlockSpec(memory_space=pltpu.VMEM)
     dma = pltpu.SemaphoreType.DMA
-    return pl.pallas_call(
+    summed = pl.pallas_call(
         kernel,
-        out_shape=(
-            jax.ShapeDtypeStruct((RANK, QCOLS), F32),
-            jax.ShapeDtypeStruct((RANK, KCOLS), F32),
-            jax.ShapeDtypeStruct((RANK, KCOLS), F32),
-        ),
+        out_shape=jax.ShapeDtypeStruct((8, RANK, HEAD_SIZE), F32),
         in_specs=[any_spec] * 9,
-        out_specs=(vmem, vmem, vmem),
+        out_specs=vmem,
         scratch_shapes=[
-            pltpu.VMEM((ROWS, WIDTH), BF16),
-            pltpu.VMEM((1, WIDTH), BF16),
+            pltpu.VMEM((WIDTH, ROWS), BF16),
+            pltpu.VMEM((WIDTH,), BF16),
             pltpu.VMEM((1, WINDOW), jnp.int32),
             pltpu.VMEM((ROWS, QCOLS), BF16),
             pltpu.VMEM((WINDOW, KCOLS), BF16),
             pltpu.VMEM((WINDOW, KCOLS), BF16),
-            pltpu.VMEM((8, QCOLS, WIDTH), BF16),
+            pltpu.VMEM((8, WIDTH, QCOLS), BF16),
+            pltpu.VMEM((WIDTH, ROWS), BF16),
             pltpu.VMEM((ROWS, WIDTH), BF16),
-            pltpu.VMEM((WIDTH, 3 * RANK), BF16),
+            pltpu.VMEM((3 * RANK, WIDTH), BF16),
             pltpu.VMEM((4, ROWS, QCOLS), BF16),
             pltpu.VMEM((4, ROWS, QCOLS), F32),
             pltpu.VMEM((4, ROWS, QCOLS), BF16),
@@ -465,7 +505,17 @@
         cost_estimate=pl.CostEstimate(
             flops=8_000_000_000, bytes_accessed=10_000_000, transcendentals=3_000_000
         ),
-    )(x, nw.reshape(1, WIDTH), doc.reshape(1, ROWS), q, k, v, w, pg, a)
+    )(x.T, nw, doc.reshape(1, ROWS), q, k, v, w.T, pg.T, a.T)
+    return pl.pallas_call(
+        split,
+        out_shape=(
+            jax.ShapeDtypeStruct((RANK, QCOLS), F32),
+            jax.ShapeDtypeStruct((RANK, KCOLS), F32),
+            jax.ShapeDtypeStruct((RANK, KCOLS), F32),
+        ),
+        in_specs=[vmem],
+        out_specs=(vmem, vmem, vmem),
+    )(summed)
 
 
 def solution(mesh):

time: 102 us -> 82.5 us (0.81); the launches traced: 100 us -> 82.4 us
  local copies, waits for them, and re-layouts: 19.6 us -> 0 us
  Pallas kernels: 80 us -> 81.7 us
    unnamed x7 -> x0, local copies, waits for them, and re-layouts: 18.3 us -> none
    pallas_call x1 -> x2, Pallas kernels: 80 us -> 81.7 us  [the longest x1 80.3 us: per_device(): pl.pallas_call(kernel, out_shape=jax.ShapeDtypeStruct((8, RANK, HEAD_SIZE...]
    reshape x1 -> x0, local copies, waits for them, and re-layouts: 1.26 us -> none  [per_device(): nw.reshape(1, WIDTH)]
where the time goes in v2:
time: 82.5 us; the launch traced here: 82.4 us
  Pallas kernels  81.7 us (99%)
    pallas_call x1, Pallas kernels, per_device(): pl.pallas_call(kernel, out_shape=jax.ShapeDtypeStruct((8, RANK, HEAD_SIZE...  80.3 us

profile of v2, /device:TPU:8, one launch (start us, length us, event | category | flops | bytes accessed | tf_op | source)
XLA Modules:
  0.0 82.4 jit_solution(6146166985005137627)
XLA Ops:
  0.6 80.3 %shard_map.112.sum_ref = f32[8,8,128]{2,1,0:T(8,128)} custom-call(bf16[672,512]{1,0:T(8,128)(2,1)} %bitcast.6, bf16[672]{0:T(1024)(128)(2,1)} %nw_ref.1, s32[1,512]{1,0:T(1,128)} %bitcast.9, bf16[512,512]{1,0:T(8,128)(2,1)} %q_ref.1, bf16[512,256]{1,0:T(8,128)(2,1)} %k_ref.1, bf16[512,256]{1,0:T(8,128)(2,1)} %v_ref.1, bf16[672,4096]{1,0:T(8,128)(2,1)} %bitcast.5, ...), custom_call_target="tpu_custom_call" | custom-call | flops 8000000000 | bytes 10000000 | tf_op jit(solution)/shard_map/pallas_call | solution.py:458
  81.0 1.4 %shard_map.113 = (f32[8,512]{1,0:T(8,128)}, f32[8,256]{1,0:T(8,128)}, f32[8,256]{1,0:T(8,128)}) custom-call(f32[8,8,128]{2,1,0:T(8,128)} %shard_map.112.sum_ref), custom_call_target="tpu_custom_call" | custom-call | tf_op jit(solution)/shard_map/pallas_call | solution.py:509

commit v3 on v2

v3 whole, which is shorter than its diff:
```python
import jax
import jax.numpy as jnp
from jax import lax
from jax.experimental import pallas as pl
from jax.experimental.pallas import tpu as pltpu
from jax.sharding import PartitionSpec as P

MODEL_WIDTH = 5376
QUERY_HEADS = 32
KEY_VALUE_HEADS = 16
HEAD_SIZE = 128
LOOKBACK_SPAN = 1024
RANK = 8

CTX = 32
ROWS = 512
WIDTH = 672
QCOLS = 512
KCOLS = 256
WINDOW = 1536
KSPAN = 1152
RC = 128
NRC = ROWS // RC
SCALE = float(MODEL_WIDTH // QUERY_HEADS) ** (-0.5)
LOG2E = 1.4426950408889634

MESH = pl.DeviceIdType.MESH
NT = (((1,), (1,)), ((), ()))
NN = (((1,), (0,)), ((), ()))
F32 = jnp.float32
BF16 = jnp.bfloat16


def dot(a, b, dims=NN):
    return lax.dot_general(a, b, dims, preferred_element_type=F32)


def loop(count, body):
    def step(i, carry):
        body(i)
        return carry

    lax.fori_loop(0, count, step, 0)


def kernel(
    x_ref, nw_ref, doc_ref, q_ref, k_ref, v_ref, w_ref, pg_ref, a_ref,
    out_ref,
    xs, nws, ids, qs, kx, vx, ws, pgt, pgs, am,
    psend, pacc, precv, asend, arecv, xsend, xrecv,
    tmine, trecv, tx_send, tx_recv, lown, lx,
    bias, probs, rv, g, acc, ar, red, fin, sq, sqr,
    load_sem, wload_sem, halo_send, halo_recv, id_send, id_recv, known,
    p_send, p_recv, a_send, a_recv, x_send, x_recv,
    t1_send, t1_recv, t2_send, t2_recv, t3_send, t3_recv, t4_send, t4_recv,
    ar_send, ar_recv, fin_send, fin_recv, sq_send, sq_recv,
):
    c = lax.axis_index("ctx")
    t = lax.axis_index("tp")
    xh = t // 4
    y = t % 4
    z = c // 4
    low = c % 4
    up = xh * 4 + (y + 1) % 4
    down = xh * 4 + (y + 3) % 4
    across = (t + 4) % 8

    def remote(src, dst, ssem, rsem, cc, tt):
        return pltpu.make_async_remote_copy(
            src_ref=src, dst_ref=dst, send_sem=ssem, recv_sem=rsem,
            device_id=(cc, tt), device_id_type=MESH,
        )

    loads = [
        pltpu.make_async_copy(src, dst, load_sem.at[n])
        for n, (src, dst) in enumerate([
            (pg_ref, pgt), (x_ref, xs), (nw_ref, nws), (a_ref, am), (q_ref, qs),
            (k_ref, kx.at[pl.ds(1024, ROWS), :]), (v_ref, vx.at[pl.ds(1024, ROWS), :]),
            (doc_ref, ids.at[:, pl.ds(1024, ROWS)]),
        ])
    ]

    def order_of(s):
        first_x = ((s + 1) // 2) % 2
        first_y = 2 + (s // 2) * ((s % 2) * 2 - 1)
        late = s - 4
        late_x = s % 2
        late_y = (1 - late // 2) * (1 + 2 * (s % 2))
        is_late = s // 4
        dx = first_x * (1 - is_late) + late_x * is_late
        dy = first_y * (1 - is_late) + late_y * is_late
        return dx * 4 + (y + dy) % 4

    def wload(s):
        cols = pl.ds(pl.multiple_of(order_of(s) * QCOLS, QCOLS), QCOLS)
        return pltpu.make_async_copy(w_ref.at[:, cols], ws.at[s], wload_sem.at[s])

    loads[0].start()
    loop(2, lambda s: wload(s).start())

    barrier = pltpu.get_barrier_semaphore()

    def greet_tp(i):
        pl.semaphore_signal(barrier, inc=1, device_id=(c, (t + 1 + i) % 8), device_id_type=MESH)

    def meet(sem, d):
        pl.semaphore_signal(sem, inc=1, device_id=((c + d) % CTX, t), device_id_type=MESH)
        pl.semaphore_signal(sem, inc=1, device_id=((c + CTX - d) % CTX, t), device_id_type=MESH)

    loop(7, greet_tp)
    meet(barrier, 1)
    meet(barrier, 2)

    for copy in loads[1:]:
        copy.start()
    loop(6, lambda s: wload(s + 2).start())

    def rows_of(rc):
        return pl.ds(pl.multiple_of(rc * RC, RC), RC)

    def p_copy(s, rc):
        turn = (y + 1 + 2 * (s % 2)) % 4
        return remote(
            psend.at[s, rows_of(rc), :], precv.at[s, rows_of(rc), :],
            p_send.at[s, rc], p_recv.at[s, rc], c, xh * 4 + turn,
        )

    def a_copy(s, rc):
        turn = (y + 1 + 2 * s) % 4
        return remote(
            asend.at[s, rows_of(rc), :], arecv.at[s, rows_of(rc), :],
            a_send.at[s, rc], a_recv.at[s, rc], c, xh * 4 + turn,
        )

    def x_copy(rc):
        return remote(
            xsend.at[rows_of(rc), :], xrecv.at[rows_of(rc), :],
            x_send.at[rc], x_recv.at[rc], c, across,
        )

    def early(s):
        wload(s).wait()
        psend[s] = dot(pgs[...], ws[s]).astype(BF16)

    def late(s):
        wload(s + 4).wait()
        pacc[s] = dot(pgs[...], ws[s + 4])

    def message(k, n):
        if k < 4:
            return p_copy(n, k)
        if k % 2 == 0:
            return p_copy(2 + n, (k - 4) // 2)
        return a_copy(n, (k - 5) // 2)

    def issue(k):
        for n in range(2):
            if k >= 2:
                message(k - 2, n).wait_send()
            message(k, n).start()

    def pass_on(rc):
        for n in range(2):
            p_copy(n, rc).wait_recv()
            asend[n, rows_of(rc), :] = (
                pacc[n, rows_of(rc), :] + precv[n, rows_of(rc), :].astype(F32)
            ).astype(BF16)

    def id_copy(d):
        return remote(
            doc_ref, ids.at[:, pl.ds((2 - d) * ROWS, ROWS)], id_send.at[d - 1], id_recv.at[d - 1],
            (c + d) % CTX, t,
        )

    def kv_copy(m, hop):
        own, window = ((k_ref, kx), (v_ref, vx))[m]
        near = window.at[pl.ds(512, ROWS), :]
        far = window.at[pl.ds(0, ROWS), :]
        return remote(
            near if hop else own, far if hop else near,
            halo_send.at[m, hop], halo_recv.at[m, hop], (c + 1) % CTX, t,
        )

    loads[0].wait()
    pgs[...] = jnp.transpose(pgt[...], (1, 0))
    loop(2, early)
    pl.semaphore_wait(barrier, 7 + 4)

    issue(0)
    kv_copy(0, 0).start()
    issue(1)
    id_copy(1).start()
    id_copy(2).start()
    meet(known.at[0], 2)

    for copy in loads[1:4]:
        copy.wait()
    sel_row = lax.broadcasted_iota(jnp.int32, (32, 3 * RANK), 0)
    sel_col = lax.broadcasted_iota(jnp.int32, (32, 3 * RANK), 1)
    wanted = jnp.where(sel_row < 16, sel_row + 8, jnp.where(sel_row < 24, sel_row - 16, -1))
    select = (wanted == sel_col).astype(BF16)
    maps = dot(select, am[...]) * nws[...].astype(F32).reshape(1, WIDTH)
    maps_hi = maps.astype(BF16)
    maps_lo = (maps - maps_hi.astype(F32)).astype(BF16)
    x_low = xs[...]
    part = dot(maps_hi, x_low) + dot(maps_lo, x_low)
    x_wide = x_low.astype(F32)
    square = x_wide * x_wide
    square_hi = square.astype(BF16)
    square_lo = (square - square_hi.astype(F32)).astype(BF16)
    ones = jnp.ones((RANK, WIDTH), BF16)
    squares = dot(ones, square_hi) + dot(ones, square_lo)
    for n in range(4):
        cols = slice(n * 128, (n + 1) * 128)
        tmine[n, 0:24, :] = part[0:24, cols]
        tmine[n, 24:32, :] = squares[:, cols]

    def t1_copy(d):
        dest = (y + d) % 4
        return remote(tmine.at[dest], trecv.at[y], t1_send.at[d], t1_recv.at[y], c, xh * 4 + dest)

    def t1_wait(d):
        src = (y + d) % 4
        remote(tmine.at[y], trecv.at[src], t1_send.at[d], t1_recv.at[src], c, t).wait_recv()
        t1_copy(d).wait_send()

    loop(3, lambda d: t1_copy(d + 1).start())

    loop(2, lambda s: early(s + 2))
    issue(2)
    loop(2, late)
    kv_copy(0, 0).wait_recv()
    kv_copy(0, 1).start()
    issue(3)
    loop(2, lambda s: late(s + 2))

    loop(3, lambda d: t1_wait(d + 1))
    tsum = tmine[y]
    for d in range(1, 4):
        tsum = tsum + trecv[(y + d) % 4]
    tx_send[...] = tsum
    t2 = remote(tx_send, tx_recv, t2_send, t2_recv, c, across)
    t2.start()
    kv_copy(1, 0).start()
    pl.semaphore_wait(known.at[0], 2)
    meet(known.at[1], 4)

    issue(4)
    pass_on(0)

    for copy in loads[4:]:
        copy.wait()
    id_copy(1).wait()
    id_copy(2).wait()
    key_at = lax.broadcasted_iota(jnp.int32, (1, WINDOW), 1) + c * ROWS - LOOKBACK_SPAN
    key_ids = jnp.where(key_at < 0, -1, ids[...]).astype(F32)
    own_ids = jnp.broadcast_to(key_ids[:, 1024:1536], (128, ROWS))
    query_ids = jnp.transpose(own_ids, (1, 0))
    row_at = lax.broadcasted_iota(jnp.int32, (RC, 128), 0)
    col_at = lax.broadcasted_iota(jnp.int32, (RC, 128), 1)
    for b in range(NRC):
        for m in range(KSPAN // 128):
            start = (b + m) * 128
            spacing = 1024 - m * 128 + row_at - col_at
            allowed = query_ids[b * RC:(b + 1) * RC, :] == key_ids[:, start:start + 128]
            allowed = allowed & (spacing >= 0) & (spacing < LOOKBACK_SPAN)
            bias[b, :, m * 128:(m + 1) * 128] = jnp.where(allowed, 0.0, -1e30)

    def parts_of(i):
        rc, group = i // 2, i % 2
        k_rows = pl.ds(pl.multiple_of(rc * RC, RC), KSPAN)
        g_cols = pl.ds(pl.multiple_of(group * HEAD_SIZE, HEAD_SIZE), HEAD_SIZE)
        return rc, group, k_rows, g_cols

    def both_heads(ref, rc, group):
        return jnp.concatenate([
            ref[rows_of(rc), pl.ds(pl.multiple_of((2 * group + n) * HEAD_SIZE, HEAD_SIZE), HEAD_SIZE)]
            for n in range(2)
        ], axis=0)

    def softmax(i):
        rc, group, k_rows, g_cols = parts_of(i)
        scores = dot(both_heads(qs, rc, group), kx[k_rows, g_cols], NT) * (SCALE * LOG2E)
        scores = (scores.reshape(2, RC, KSPAN) + bias[rc][None]).reshape(2 * RC, KSPAN)
        highest = jnp.max(scores, axis=-1, keepdims=True)
        expons = jnp.exp2(scores - highest)
        total = jnp.sum(expons, axis=-1, keepdims=True)
        probs[i] = expons * (1.0 / total)

    def value_side(i):
        rc, group, k_rows, g_cols = parts_of(i)
        rv[i] = dot(lx[0:16, k_rows], probs[i].astype(BF16), NT)

    def finish(rc):
        rows = rows_of(rc)
        for n in range(2):
            p_copy(2 + n, rc).wait_recv()
            a_copy(n, rc).wait_recv()
        xsend[rows, :] = (
            pacc[3 - xh, rows, :] + arecv[1 - xh, rows, :].astype(F32)
            + precv[2 + xh, rows, :].astype(F32)
        ).astype(BF16)
        x_copy(rc).start()
        pacc[2 + xh, rows, :] = (
            pacc[2 + xh, rows, :] + arecv[xh, rows, :].astype(F32)
            + precv[3 - xh, rows, :].astype(F32)
        )

    def take(rc):
        rows = rows_of(rc)
        x_copy(rc).wait_recv()
        g[rows, :] = (pacc[2 + xh, rows, :] + xrecv[rows, :].astype(F32)).astype(BF16)

    def backward(i):
        rc, group, k_rows, g_cols = parts_of(i)
        grad = both_heads(g, rc, group)
        grad_probs = dot(grad, vx[k_rows, g_cols], NT)
        prob = probs[i]
        delta = jnp.sum(prob * grad_probs, axis=-1, keepdims=True)
        grad_scores = (prob * (grad_probs - delta)).astype(BF16)
        side_k = (dot(lx[0:16, k_rows], grad_scores, NT) * SCALE).astype(BF16)
        own = lx[16:32, pl.ds(pl.multiple_of(1024 + rc * RC, RC), RC)]
        none = jnp.zeros_like(own)
        own_both = jnp.concatenate([
            jnp.concatenate([own, none], axis=1), jnp.concatenate([none, own], axis=1)
        ], axis=0)
        side_q = (dot(own_both, grad_scores) * SCALE).astype(BF16)
        to_q = dot(side_q, kx[k_rows, g_cols])
        acc[2 * group] += to_q[0:8]
        acc[2 * group + 1] += to_q[16:24]
        acc[4 + group] += dot(side_k, both_heads(qs, rc, group))[0:8]
        acc[6 + group] += dot(rv[i].astype(BF16), grad)[8:16]

    acc[...] = jnp.zeros_like(acc)
    issue(5)
    kv_copy(0, 1).wait_recv()
    loop(2, softmax)
    pass_on(1)
    issue(6)

    t2.wait()
    tfull = tx_send[...] + tx_recv[...]
    rstd = lax.rsqrt(tfull[24:32, :] * (1.0 / MODEL_WIDTH) + 1e-06)
    lown[...] = (tfull * jnp.concatenate([rstd] * 4, axis=0)).astype(BF16)

    def own_cols(n):
        return pl.ds(pl.multiple_of(1024 + n * 128, 128), 128)

    lx[:, own_cols(y)] = lown[...]

    def t3_copy(d):
        return remote(
            lown, lx.at[:, own_cols(y)], t3_send.at[d], t3_recv.at[y], c, xh * 4 + (y + d) % 4
        )

    def t3_wait(d):
        src = (y + d) % 4
        remote(lown, lx.at[:, own_cols(src)], t3_send.at[d], t3_recv.at[src], c, t).wait_recv()
        t3_copy(d).wait_send()

    loop(3, lambda d: t3_copy(d + 1).start())
    pl.semaphore_wait(known.at[1], 2)
    meet(known.at[2], 8)

    loop(2, lambda i: softmax(i + 2))
    kv_copy(1, 0).wait_recv()
    kv_copy(1, 1).start()
    issue(7)
    loop(2, lambda i: softmax(i + 4))
    pass_on(2)
    issue(8)

    loop(3, lambda d: t3_wait(d + 1))
    t4s = [
        remote(
            lx.at[pl.ds(0, 16), pl.ds(1024, ROWS)], lx.at[pl.ds(0, 16), pl.ds((1 - n) * ROWS, ROWS)],
            t4_send.at[n], t4_recv.at[n], (c + n + 1) % CTX, t,
        )
        for n in range(2)
    ]
    for copy in t4s:
        copy.start()

    loop(2, lambda i: softmax(i + 6))
    finish(0)
    pass_on(3)
    issue(9)
    issue(10)
    finish(1)
    issue(11)
    for copy in t4s:
        copy.wait()
    kv_copy(1, 1).wait_recv()
    loop(4, value_side)
    take(0)
    loop(2, backward)
    finish(2)
    take(1)
    loop(2, lambda i: backward(i + 2))
    loop(4, lambda i: value_side(i + 4))
    take(2)
    finish(3)
    loop(2, lambda i: backward(i + 4))
    take(3)
    loop(2, lambda i: backward(i + 6))
    pl.semaphore_wait(known.at[2], 2)

    def ar_copy(d):
        dest = (c + d) % CTX
        return remote(acc.at[dest // 4], ar.at[c], ar_send.at[d], ar_recv.at[c], dest, t)

    def ar_wait(d):
        src = (c + d) % CTX
        remote(acc.at[z], ar.at[src], ar_send.at[d], ar_recv.at[src], c, t).wait_recv()

    loop(CTX - 1, lambda i: ar_copy(16 + (i + 1) // 2 * (2 * (i % 2) - 1)).start())
    ar[c] = acc[z]
    loop(CTX - 1, lambda d: ar_wait(d + 1))
    red[...] = jnp.sum(ar[...], axis=0)

    def fin_copy(d):
        return remote(
            red, fin.at[z], fin_send.at[d], fin_recv.at[z], ((z + d) % 8) * 4 + low, t
        )

    def fin_wait(d):
        src = (z + d) % 8
        remote(red, fin.at[src], fin_send.at[d], fin_recv.at[src], c, t).wait_recv()

    loop(7, lambda i: fin_copy(4 + (i + 1) // 2 * (2 * (i % 2) - 1)).start())
    fin[z] = red[...]
    loop(7, lambda d: fin_wait(d + 1))

    whole = fin[...]
    sq[...] = jnp.sum(whole * whole, axis=0)

    def sq_copy(d):
        return remote(sq, sqr.at[t], sq_send.at[d], sq_recv.at[t], c, (t + d) % 8)

    def sq_wait(d):
        src = (t + d) % 8
        remote(sq, sqr.at[src], sq_send.at[d], sq_recv.at[src], c, t).wait_recv()

    loop(7, lambda d: sq_copy(d + 1).start())
    sqr[t] = sq[...]
    loop(7, lambda d: sq_wait(d + 1))
    squared = jnp.sum(jnp.sum(jnp.sum(sqr[...], axis=0), axis=0, keepdims=True), axis=1, keepdims=True)
    factor = jnp.sqrt(
        float(RANK * (QUERY_HEADS + 2 * KEY_VALUE_HEADS) * HEAD_SIZE) / (squared + 1e-06)
    )
    out_ref[...] = fin[...] * factor

    for k in range(10, 12):
        for n in range(2):
            message(k, n).wait_send()
    for n in range(4):
        kv_copy(n // 2, n % 2).wait_send()
    loop(NRC, lambda rc: x_copy(rc).wait_send())
    loop(CTX - 1, lambda d: ar_copy(d + 1).wait_send())
    loop(7, lambda d: fin_copy(d + 1).wait_send())
    loop(7, lambda d: sq_copy(d + 1).wait_send())


def split(sum_ref, oq_ref, ok_ref, ov_ref):
    for n in range(4):
        oq_ref[:, n * 128:(n + 1) * 128] = sum_ref[n]
    for n in range(2):
        ok_ref[:, n * 128:(n + 1) * 128] = sum_ref[4 + n]
        ov_ref[:, n * 128:(n + 1) * 128] = sum_ref[6 + n]


def per_device(x, nw, doc, q, k, v, w, pg, a):
    any_spec = pl.BlockSpec(memory_space=pl.ANY)
    vmem = pl.BlockSpec(memory_space=pltpu.VMEM)
    dma = pltpu.SemaphoreType.DMA
    summed = pl.pallas_call(
        kernel,
        out_shape=jax.ShapeDtypeStruct((8, RANK, HEAD_SIZE), F32),
        in_specs=[any_spec] * 9,
        out_specs=vmem,
        scratch_shapes=[
            pltpu.VMEM((WIDTH, ROWS), BF16),
            pltpu.VMEM((WIDTH,), BF16),
            pltpu.VMEM((1, WINDOW), jnp.int32),
            pltpu.VMEM((ROWS, QCOLS), BF16),
            pltpu.VMEM((WINDOW, KCOLS), BF16),
            pltpu.VMEM((WINDOW, KCOLS), BF16),
            pltpu.VMEM((8, WIDTH, QCOLS), BF16),
            pltpu.VMEM((WIDTH, ROWS), BF16),
            pltpu.VMEM((ROWS, WIDTH), BF16),
            pltpu.VMEM((3 * RANK, WIDTH), BF16),
            pltpu.VMEM((4, ROWS, QCOLS), BF16),
            pltpu.VMEM((4, ROWS, QCOLS), F32),
            pltpu.VMEM((4, ROWS, QCOLS), BF16),
            pltpu.VMEM((2, ROWS, QCOLS), BF16),
            pltpu.VMEM((2, ROWS, QCOLS), BF16),
            pltpu.VMEM((ROWS, QCOLS), BF16),
            pltpu.VMEM((ROWS, QCOLS), BF16),
            pltpu.VMEM((4, 32, 128), F32),
            pltpu.VMEM((4, 32, 128), F32),
            pltpu.VMEM((32, 128), F32),
            pltpu.VMEM((32, 128), F32),
            pltpu.VMEM((32, 128), BF16),
            pltpu.VMEM((32, WINDOW), BF16),
            pltpu.VMEM((NRC, RC, KSPAN), F32),
            pltpu.VMEM((8, 2 * RC, KSPAN), F32),
            pltpu.VMEM((8, 16, 2 * RC), F32),
            pltpu.VMEM((ROWS, QCOLS), BF16),
            pltpu.VMEM((8, RANK, 128), F32),
            pltpu.VMEM((CTX, RANK, 128), F32),
            pltpu.VMEM((RANK, 128), F32),
            pltpu.VMEM((8, RANK, 128), F32),
            pltpu.VMEM((RANK, 128), F32),
            pltpu.VMEM((8, RANK, 128), F32),
            dma((8,)), dma((8,)), dma((2, 2)), dma((2, 2)), dma((2,)), dma((2,)),
            pltpu.SemaphoreType.REGULAR((3,)),
            dma((4, NRC)), dma((4, NRC)), dma((2, NRC)), dma((2, NRC)), dma((NRC,)), dma((NRC,)),
            dma((4,)), dma((4,)), dma, dma, dma((4,)), dma((4,)), dma((2,)), dma((2,)),
            dma((CTX,)), dma((CTX,)), dma((8,)), dma((8,)), dma((8,)), dma((8,)),
        ],
        compiler_params=pltpu.CompilerParams(
            collective_id=0, has_side_effects=True, vmem_limit_bytes=60 * 1024 * 1024
        ),
        cost_estimate=pl.CostEstimate(
            flops=8_000_000_000, bytes_accessed=10_000_000, transcendentals=3_000_000
        ),
    )(x.T, nw, doc.reshape(1, ROWS), q, k, v, w.T, pg.T, a.T)
    return pl.pallas_call(
        split,
        out_shape=(
            jax.ShapeDtypeStruct((RANK, QCOLS), F32),
            jax.ShapeDtypeStruct((RANK, KCOLS), F32),
            jax.ShapeDtypeStruct((RANK, KCOLS), F32),
        ),
        in_specs=[vmem],
        out_specs=(vmem, vmem, vmem),
    )(summed)


def solution(mesh):
    placed = (
        P("ctx", "tp"),
        P("tp"),
        P("ctx"),
        P("ctx", "tp"),
        P("ctx", "tp"),
        P("ctx", "tp"),
        P(None, "tp"),
        P("ctx", "tp"),
        P("tp", None),
    )
    return jax.shard_map(
        per_device,
        mesh=mesh,
        in_specs=placed,
        out_specs=(P(None, "tp"), P(None, "tp"), P(None, "tp")),
        check_vma=False,
    )
```

time: 82.5 us -> 73.2 us (0.89)
  Pallas kernels: 81.7 us -> 72.2 us
    pallas_call x1, Pallas kernels: 80.3 us -> 70.9 us  [per_device(): pl.pallas_call(kernel, out_shape=jax.ShapeDtypeStruct((8, RANK, HEAD_SIZE...]
where the time goes in v3:
time: 73.2 us; the launch traced here: 72.9 us
  Pallas kernels  72.2 us (99%)
    pallas_call x1, Pallas kernels, per_device(): pl.pallas_call(kernel, out_shape=jax.ShapeDtypeStruct((8, RANK, HEAD_SIZE...  70.9 us

profile of v3, /device:TPU:8, one launch (start us, length us, event | category | flops | bytes accessed | tf_op | source)
XLA Modules:
  0.0 72.9 jit_solution(10778719266582115953)
XLA Ops:
  0.6 70.9 %shard_map.112.sum_ref = f32[8,8,128]{2,1,0:T(8,128)} custom-call(bf16[672,512]{1,0:T(8,128)(2,1)} %bitcast.6, bf16[672]{0:T(1024)(128)(2,1)} %nw_ref.1, s32[1,512]{1,0:T(1,128)} %bitcast.9, bf16[512,512]{1,0:T(8,128)(2,1)} %q_ref.1, bf16[512,256]{1,0:T(8,128)(2,1)} %k_ref.1, bf16[512,256]{1,0:T(8,128)(2,1)} %v_ref.1, bf16[672,4096]{1,0:T(8,128)(2,1)} %bitcast.5, ...), custom_call_target="tpu_custom_call" | custom-call | flops 8000000000 | bytes 10000000 | tf_op jit(solution)/shard_map/pallas_call | solution.py:476
  71.5 1.4 %shard_map.113 = (f32[8,512]{1,0:T(8,128)}, f32[8,256]{1,0:T(8,128)}, f32[8,256]{1,0:T(8,128)}) custom-call(f32[8,8,128]{2,1,0:T(8,128)} %shard_map.112.sum_ref), custom_call_target="tpu_custom_call" | custom-call | tf_op jit(solution)/shard_map/pallas_call | solution.py:528

commit v4 on v3

--- a/solution.py
+++ b/solution.py
@@ -48,9 +48,11 @@
     out_ref,
     xs, nws, ids, qs, kx, vx, ws, pgt, pgs, am,
     psend, pacc, precv, asend, arecv, xsend, xrecv,
+    bsend, zrecv, zbuf, ssend, srecv, fsend, frecv,
     tmine, trecv, tx_send, tx_recv, lown, lx,
     bias, probs, rv, g, acc, ar, red, fin, sq, sqr,
     load_sem, wload_sem, halo_send, halo_recv, id_send, id_recv, known,
+    z_send, z_recv, s_send, s_recv, f_send, f_recv,
     p_send, p_recv, a_send, a_recv, x_send, x_recv,
     t1_send, t1_recv, t2_send, t2_recv, t3_send, t3_recv, t4_send, t4_recv,
     ar_send, ar_recv, fin_send, fin_recv, sq_send, sq_recv,
@@ -71,6 +73,23 @@
             device_id=(cc, tt), device_id_type=MESH,
         )
 
+    barrier = pltpu.get_barrier_semaphore()
+
+    def greet_y(d):
+        pl.semaphore_signal(
+            barrier, inc=1, device_id=(c, xh * 4 + (y + d) % 4), device_id_type=MESH
+        )
+
+    def meet(sem, d):
+        pl.semaphore_signal(sem, inc=1, device_id=((c + d) % CTX, t), device_id_type=MESH)
+        pl.semaphore_signal(sem, inc=1, device_id=((c + CTX - d) % CTX, t), device_id_type=MESH)
+
+    for d in (2, 1, 3):
+        greet_y(d)
+    pl.semaphore_signal(barrier, inc=1, device_id=(c, across), device_id_type=MESH)
+    meet(barrier, 1)
+    meet(barrier, 2)
+
     loads = [
         pltpu.make_async_copy(src, dst, load_sem.at[n])
         for n, (src, dst) in enumerate([
@@ -98,19 +117,6 @@
     loads[0].start()
     loop(2, lambda s: wload(s).start())
 
-    barrier = pltpu.get_barrier_semaphore()
-
-    def greet_tp(i):
-        pl.semaphore_signal(barrier, inc=1, device_id=(c, (t + 1 + i) % 8), device_id_type=MESH)
-
-    def meet(sem, d):
-        pl.semaphore_signal(sem, inc=1, device_id=((c + d) % CTX, t), device_id_type=MESH)
-        pl.semaphore_signal(sem, inc=1, device_id=((c + CTX - d) % CTX, t), device_id_type=MESH)
-
-    loop(7, greet_tp)
-    meet(barrier, 1)
-    meet(barrier, 2)
-
     for copy in loads[1:]:
         copy.start()
     loop(6, lambda s: wload(s + 2).start())
@@ -146,12 +152,35 @@
         wload(s + 4).wait()
         pacc[s] = dot(pgs[...], ws[s + 4])
 
+    last = pl.ds((NRC - 1) * RC, RC)
+
+    def x_part(m):
+        src = (
+            psend.at[1 - xh, last, :], psend.at[2 + xh, last, :], bsend.at[0], bsend.at[1]
+        )[m]
+        slot = (0, 1 + xh, 2 - xh, 3)[m]
+        return remote(src, zrecv.at[slot], z_send.at[m], z_recv.at[slot], c, across)
+
+    def x_part_wait(slot):
+        remote(bsend.at[0], zrecv.at[slot], z_send.at[0], z_recv.at[slot], c, t).wait_recv()
+
+    def s_copy(n):
+        return remote(
+            ssend.at[n], srecv.at[n], s_send.at[n], s_recv.at[n], c, xh * 4 + (y + 1 + 2 * n) % 4
+        )
+
+    def f_copy(n):
+        return remote(
+            fsend.at[n], frecv.at[n], f_send.at[n], f_recv.at[n], c, xh * 4 + (y + 1 + 2 * n) % 4
+        )
+
     def message(k, n):
-        if k < 4:
-            return p_copy(n, k)
-        if k % 2 == 0:
-            return p_copy(2 + n, (k - 4) // 2)
-        return a_copy(n, (k - 5) // 2)
+        return (
+            lambda: p_copy(n, 0), lambda: p_copy(n, 1), lambda: p_copy(n, 2),
+            lambda: p_copy(2 + n, 0), lambda: a_copy(n, 0), lambda: s_copy(n),
+            lambda: p_copy(2 + n, 1), lambda: a_copy(n, 1),
+            lambda: p_copy(2 + n, 2), lambda: a_copy(n, 2), lambda: f_copy(n),
+        )[k]()
 
     def issue(k):
         for n in range(2):
@@ -184,14 +213,16 @@
     loads[0].wait()
     pgs[...] = jnp.transpose(pgt[...], (1, 0))
     loop(2, early)
-    pl.semaphore_wait(barrier, 7 + 4)
+    pl.semaphore_wait(barrier, 4 + 4)
 
     issue(0)
+    x_part(0).start()
     kv_copy(0, 0).start()
     issue(1)
     id_copy(1).start()
     id_copy(2).start()
     meet(known.at[0], 2)
+    pl.semaphore_signal(known.at[3], inc=1, device_id=(c, across), device_id_type=MESH)
 
     for copy in loads[1:4]:
         copy.wait()
@@ -229,10 +260,7 @@
     loop(2, lambda s: early(s + 2))
     issue(2)
     loop(2, late)
-    kv_copy(0, 0).wait_recv()
-    kv_copy(0, 1).start()
-    issue(3)
-    loop(2, lambda s: late(s + 2))
+    bsend[0] = pacc[1 - xh, last, :].astype(BF16)
 
     loop(3, lambda d: t1_wait(d + 1))
     tsum = tmine[y]
@@ -241,13 +269,41 @@
     tx_send[...] = tsum
     t2 = remote(tx_send, tx_recv, t2_send, t2_recv, c, across)
     t2.start()
-    kv_copy(1, 0).start()
+    loop(2, lambda s: late(s + 2))
+    bsend[1] = pacc[3 - xh, last, :].astype(BF16)
+    kv_copy(0, 0).wait_recv()
+    kv_copy(0, 1).start()
+    issue(3)
+    x_part(1).start()
+    x_part(2).start()
     pl.semaphore_wait(known.at[0], 2)
     meet(known.at[1], 4)
-
+    pass_on(0)
     issue(4)
-    pass_on(0)
-
+    x_part(3).start()
+    kv_copy(1, 0).start()
+
+    t2.wait()
+    tfull = tx_send[...] + tx_recv[...]
+    rstd = lax.rsqrt(tfull[24:32, :] * (1.0 / MODEL_WIDTH) + 1e-06)
+    lown[...] = (tfull * jnp.concatenate([rstd] * 4, axis=0)).astype(BF16)
+
+    def own_cols(n):
+        return pl.ds(pl.multiple_of(1024 + n * 128, 128), 128)
+
+    lx[:, own_cols(y)] = lown[...]
+
+    def t3_copy(d):
+        return remote(
+            lown, lx.at[:, own_cols(y)], t3_send.at[d], t3_recv.at[y], c, xh * 4 + (y + d) % 4
+        )
+
+    def t3_wait(d):
+        src = (y + d) % 4
+        remote(lown, lx.at[:, own_cols(src)], t3_send.at[d], t3_recv.at[src], c, t).wait_recv()
+        t3_copy(d).wait_send()
+
+    loop(3, lambda d: t3_copy(d + 1).start())
     for copy in loads[4:]:
         copy.wait()
     id_copy(1).wait()
@@ -332,36 +388,29 @@
         acc[6 + group] += dot(rv[i].astype(BF16), grad)[8:16]
 
     acc[...] = jnp.zeros_like(acc)
+    x_part_wait(0)
+    far = psend[xh, last, :].astype(F32) + zrecv[0].astype(F32)
+    ssend[0] = far[:, 0:256].astype(BF16)
+    ssend[1] = far[:, 256:512].astype(BF16)
     issue(5)
     kv_copy(0, 1).wait_recv()
     loop(2, softmax)
     pass_on(1)
     issue(6)
 
-    t2.wait()
-    tfull = tx_send[...] + tx_recv[...]
-    rstd = lax.rsqrt(tfull[24:32, :] * (1.0 / MODEL_WIDTH) + 1e-06)
-    lown[...] = (tfull * jnp.concatenate([rstd] * 4, axis=0)).astype(BF16)
-
-    def own_cols(n):
-        return pl.ds(pl.multiple_of(1024 + n * 128, 128), 128)
-
-    lx[:, own_cols(y)] = lown[...]
-
-    def t3_copy(d):
-        return remote(
-            lown, lx.at[:, own_cols(y)], t3_send.at[d], t3_recv.at[y], c, xh * 4 + (y + d) % 4
-        )
-
-    def t3_wait(d):
-        src = (y + d) % 4
-        remote(lown, lx.at[:, own_cols(src)], t3_send.at[d], t3_recv.at[src], c, t).wait_recv()
-        t3_copy(d).wait_send()
-
-    loop(3, lambda d: t3_copy(d + 1).start())
+    loop(3, lambda d: t3_wait(d + 1))
+    t4s = [
+        remote(
+            lx.at[pl.ds(0, 16), pl.ds(1024, ROWS)], lx.at[pl.ds(0, 16), pl.ds((1 - n) * ROWS, ROWS)],
+            t4_send.at[n], t4_recv.at[n], (c + n + 1) % CTX, t,
+        )
+        for n in range(2)
+    ]
+    for copy in t4s:
+        copy.start()
+
     pl.semaphore_wait(known.at[1], 2)
     meet(known.at[2], 8)
-
     loop(2, lambda i: softmax(i + 2))
     kv_copy(1, 0).wait_recv()
     kv_copy(1, 1).start()
@@ -369,41 +418,42 @@
     loop(2, lambda i: softmax(i + 4))
     pass_on(2)
     issue(8)
-
-    loop(3, lambda d: t3_wait(d + 1))
-    t4s = [
-        remote(
-            lx.at[pl.ds(0, 16), pl.ds(1024, ROWS)], lx.at[pl.ds(0, 16), pl.ds((1 - n) * ROWS, ROWS)],
-            t4_send.at[n], t4_recv.at[n], (c + n + 1) % CTX, t,
-        )
-        for n in range(2)
-    ]
-    for copy in t4s:
-        copy.start()
-
+    finish(0)
     loop(2, lambda i: softmax(i + 6))
-    finish(0)
-    pass_on(3)
+
+    for slot in range(1, 4):
+        x_part_wait(slot)
+    zbuf[2 - xh] = psend[3 - xh, last, :].astype(F32) + zrecv[2 - xh].astype(F32)
+    zbuf[1 + xh] = pacc[xh, last, :] + zrecv[1 + xh].astype(F32)
+    zbuf[3] = pacc[2 + xh, last, :] + zrecv[3].astype(F32)
+    for n in range(2):
+        s_copy(n).wait_recv()
+        passed = slice(n * 256, (n + 1) * 256)
+        direct = slice((1 - n) * 256, (2 - n) * 256)
+        fsend[n, :, passed] = (zbuf[1 + n, :, passed] + srecv[n].astype(F32)).astype(BF16)
+        fsend[n, :, direct] = zbuf[1 + n, :, direct].astype(BF16)
+
     issue(9)
-    issue(10)
-    finish(1)
-    issue(11)
     for copy in t4s:
         copy.wait()
+    loop(4, value_side)
     kv_copy(1, 1).wait_recv()
-    loop(4, value_side)
+    issue(10)
     take(0)
+    finish(1)
     loop(2, backward)
+    loop(4, lambda i: value_side(i + 4))
     finish(2)
     take(1)
     loop(2, lambda i: backward(i + 2))
-    loop(4, lambda i: value_side(i + 4))
+    for n in range(2):
+        f_copy(n).wait_recv()
+    g[last, :] = (zbuf[3] + frecv[0].astype(F32) + frecv[1].astype(F32)).astype(BF16)
+    loop(2, lambda i: backward(i + 6))
     take(2)
-    finish(3)
     loop(2, lambda i: backward(i + 4))
-    take(3)
-    loop(2, lambda i: backward(i + 6))
     pl.semaphore_wait(known.at[2], 2)
+    pl.semaphore_wait(known.at[3], 1)
 
     def ar_copy(d):
         dest = (c + d) % CTX
@@ -418,6 +468,9 @@
     loop(CTX - 1, lambda d: ar_wait(d + 1))
     red[...] = jnp.sum(ar[...], axis=0)
 
+    def spread(i):
+        return 4 + (i + 1) // 2 * (2 * (i % 2) - 1)
+
     def fin_copy(d):
         return remote(
             red, fin.at[z], fin_send.at[d], fin_recv.at[z], ((z + d) % 8) * 4 + low, t
@@ -427,7 +480,7 @@
         src = (z + d) % 8
         remote(red, fin.at[src], fin_send.at[d], fin_recv.at[src], c, t).wait_recv()
 
-    loop(7, lambda i: fin_copy(4 + (i + 1) // 2 * (2 * (i % 2) - 1)).start())
+    loop(7, lambda i: fin_copy(spread(i)).start())
     fin[z] = red[...]
     loop(7, lambda d: fin_wait(d + 1))
 
@@ -450,12 +503,14 @@
     )
     out_ref[...] = fin[...] * factor
 
-    for k in range(10, 12):
+    for k in range(9, 11):
         for n in range(2):
             message(k, n).wait_send()
     for n in range(4):
         kv_copy(n // 2, n % 2).wait_send()
-    loop(NRC, lambda rc: x_copy(rc).wait_send())
+    for m in range(4):
+        x_part(m).wait_send()
+    loop(NRC - 1, lambda rc: x_copy(rc).wait_send())
     loop(CTX - 1, lambda d: ar_copy(d + 1).wait_send())
     loop(7, lambda d: fin_copy(d + 1).wait_send())
     loop(7, lambda d: sq_copy(d + 1).wait_send())
@@ -496,6 +551,13 @@
             pltpu.VMEM((2, ROWS, QCOLS), BF16),
             pltpu.VMEM((ROWS, QCOLS), BF16),
             pltpu.VMEM((ROWS, QCOLS), BF16),
+            pltpu.VMEM((2, RC, QCOLS), BF16),
+            pltpu.VMEM((4, RC, QCOLS), BF16),
+            pltpu.VMEM((4, RC, QCOLS), F32),
+            pltpu.VMEM((2, RC, QCOLS // 2), BF16),
+            pltpu.VMEM((2, RC, QCOLS // 2), BF16),
+            pltpu.VMEM((2, RC, QCOLS), BF16),
+            pltpu.VMEM((2, RC, QCOLS), BF16),
             pltpu.VMEM((4, 32, 128), F32),
             pltpu.VMEM((4, 32, 128), F32),
             pltpu.VMEM((32, 128), F32),
@@ -513,7 +575,8 @@
             pltpu.VMEM((RANK, 128), F32),
             pltpu.VMEM((8, RANK, 128), F32),
             dma((8,)), dma((8,)), dma((2, 2)), dma((2, 2)), dma((2,)), dma((2,)),
-            pltpu.SemaphoreType.REGULAR((3,)),
+            pltpu.SemaphoreType.REGULAR((4,)),
+            dma((4,)), dma((4,)), dma((2,)), dma((2,)), dma((2,)), dma((2,)),
             dma((4, NRC)), dma((4, NRC)), dma((2, NRC)), dma((2, NRC)), dma((NRC,)), dma((NRC,)),
             dma((4,)), dma((4,)), dma, dma, dma((4,)), dma((4,)), dma((2,)), dma((2,)),
             dma((CTX,)), dma((CTX,)), dma((8,)), dma((8,)), dma((8,)), dma((8,)),

time: 73.2 us -> 70.9 us (0.969)
  Pallas kernels: 72.2 us -> 69.7 us
    pallas_call x1, Pallas kernels: 70.9 us -> 68.3 us  [per_device(): pl.pallas_call(kernel, out_shape=jax.ShapeDtypeStruct((8, RANK, HEAD_SIZE...]
where the time goes in v4:
time: 70.9 us; the launch traced here: 70.4 us
  Pallas kernels  69.7 us (98%)
    pallas_call x1, Pallas kernels, per_device(): pl.pallas_call(kernel, out_shape=jax.ShapeDtypeStruct((8, RANK, HEAD_SIZE...  68.3 us

profile of v4, /device:TPU:8, one launch (start us, length us, event | category | flops | bytes accessed | tf_op | source)
XLA Modules:
  0.0 70.4 jit_solution(17970285294017453356)
XLA Ops:
  0.6 68.3 %shard_map.112.sum_ref = f32[8,8,128]{2,1,0:T(8,128)} custom-call(bf16[672,512]{1,0:T(8,128)(2,1)} %bitcast.6, bf16[672]{0:T(1024)(128)(2,1)} %nw_ref.1, s32[1,512]{1,0:T(1,128)} %bitcast.9, bf16[512,512]{1,0:T(8,128)(2,1)} %q_ref.1, bf16[512,256]{1,0:T(8,128)(2,1)} %k_ref.1, bf16[512,256]{1,0:T(8,128)(2,1)} %v_ref.1, bf16[672,4096]{1,0:T(8,128)(2,1)} %bitcast.5, ...), custom_call_target="tpu_custom_call" | custom-call | flops 8000000000 | bytes 10000000 | tf_op jit(solution)/shard_map/pallas_call | solution.py:531
  69.0 1.4 %shard_map.113 = (f32[8,512]{1,0:T(8,128)}, f32[8,256]{1,0:T(8,128)}, f32[8,256]{1,0:T(8,128)}) custom-call(f32[8,8,128]{2,1,0:T(8,128)} %shard_map.112.sum_ref), custom_call_target="tpu_custom_call" | custom-call | tf_op jit(solution)/shard_map/pallas_call | solution.py:591

commit v5 on v4

--- a/solution.py
+++ b/solution.py
@@ -73,23 +73,6 @@
             device_id=(cc, tt), device_id_type=MESH,
         )
 
-    barrier = pltpu.get_barrier_semaphore()
-
-    def greet_y(d):
-        pl.semaphore_signal(
-            barrier, inc=1, device_id=(c, xh * 4 + (y + d) % 4), device_id_type=MESH
-        )
-
-    def meet(sem, d):
-        pl.semaphore_signal(sem, inc=1, device_id=((c + d) % CTX, t), device_id_type=MESH)
-        pl.semaphore_signal(sem, inc=1, device_id=((c + CTX - d) % CTX, t), device_id_type=MESH)
-
-    for d in (2, 1, 3):
-        greet_y(d)
-    pl.semaphore_signal(barrier, inc=1, device_id=(c, across), device_id_type=MESH)
-    meet(barrier, 1)
-    meet(barrier, 2)
-
     loads = [
         pltpu.make_async_copy(src, dst, load_sem.at[n])
         for n, (src, dst) in enumerate([
@@ -117,9 +100,23 @@
     loads[0].start()
     loop(2, lambda s: wload(s).start())
 
-    for copy in loads[1:]:
-        copy.start()
-    loop(6, lambda s: wload(s + 2).start())
+    barrier = pltpu.get_barrier_semaphore()
+
+    def greet_y(d):
+        pl.semaphore_signal(
+            barrier, inc=1, device_id=(c, xh * 4 + (y + d) % 4), device_id_type=MESH
+        )
+
+    def meet(sem, d):
+        pl.semaphore_signal(sem, inc=1, device_id=((c + d) % CTX, t), device_id_type=MESH)
+        pl.semaphore_signal(sem, inc=1, device_id=((c + CTX - d) % CTX, t), device_id_type=MESH)
+
+    for d in (2, 1, 3):
+        greet_y(d)
+    pl.semaphore_signal(barrier, inc=1, device_id=(c, across), device_id_type=MESH)
+    meet(barrier, 1)
+    meet(barrier, 2)
+
 
     def rows_of(rc):
         return pl.ds(pl.multiple_of(rc * RC, RC), RC)
@@ -184,8 +181,8 @@
 
     def issue(k):
         for n in range(2):
-            if k >= 2:
-                message(k - 2, n).wait_send()
+            if k >= 4:
+                message(k - 4, n).wait_send()
             message(k, n).start()
 
     def pass_on(rc):
@@ -211,16 +208,31 @@
         )
 
     loads[0].wait()
-    pgs[...] = jnp.transpose(pgt[...], (1, 0))
-    loop(2, early)
+    pgs[0:RC, :] = jnp.transpose(pgt[:, 0:RC], (1, 0))
+
+    def first(s):
+        wload(s).wait()
+        psend[s, 0:RC, :] = dot(pgs[0:RC, :], ws[s]).astype(BF16)
+
+    loop(2, first)
     pl.semaphore_wait(barrier, 4 + 4)
 
     issue(0)
+    for copy in loads[1:]:
+        copy.start()
+    loop(6, lambda s: wload(s + 2).start())
+    pgs[RC:ROWS, :] = jnp.transpose(pgt[:, RC:ROWS], (1, 0))
+
+    def second(s):
+        psend[s, RC:ROWS, :] = dot(pgs[RC:ROWS, :], ws[s]).astype(BF16)
+
+    loop(2, second)
     x_part(0).start()
     kv_copy(0, 0).start()
     issue(1)
     id_copy(1).start()
     id_copy(2).start()
+    kv_copy(1, 0).start()
     meet(known.at[0], 2)
     pl.semaphore_signal(known.at[3], inc=1, device_id=(c, across), device_id_type=MESH)
 
@@ -271,9 +283,9 @@
     t2.start()
     loop(2, lambda s: late(s + 2))
     bsend[1] = pacc[3 - xh, last, :].astype(BF16)
+    issue(3)
     kv_copy(0, 0).wait_recv()
     kv_copy(0, 1).start()
-    issue(3)
     x_part(1).start()
     x_part(2).start()
     pl.semaphore_wait(known.at[0], 2)
@@ -281,7 +293,6 @@
     pass_on(0)
     issue(4)
     x_part(3).start()
-    kv_copy(1, 0).start()
 
     t2.wait()
     tfull = tx_send[...] + tx_recv[...]
@@ -393,6 +404,8 @@
     ssend[0] = far[:, 0:256].astype(BF16)
     ssend[1] = far[:, 256:512].astype(BF16)
     issue(5)
+    kv_copy(1, 0).wait_recv()
+    kv_copy(1, 1).start()
     kv_copy(0, 1).wait_recv()
     loop(2, softmax)
     pass_on(1)
@@ -412,8 +425,6 @@
     pl.semaphore_wait(known.at[1], 2)
     meet(known.at[2], 8)
     loop(2, lambda i: softmax(i + 2))
-    kv_copy(1, 0).wait_recv()
-    kv_copy(1, 1).start()
     issue(7)
     loop(2, lambda i: softmax(i + 4))
     pass_on(2)
@@ -434,11 +445,11 @@
         fsend[n, :, direct] = zbuf[1 + n, :, direct].astype(BF16)
 
     issue(9)
+    issue(10)
     for copy in t4s:
         copy.wait()
     loop(4, value_side)
     kv_copy(1, 1).wait_recv()
-    issue(10)
     take(0)
     finish(1)
     loop(2, backward)
@@ -465,45 +476,7 @@
 
     loop(CTX - 1, lambda i: ar_copy(16 + (i + 1) // 2 * (2 * (i % 2) - 1)).start())
     ar[c] = acc[z]
-    loop(CTX - 1, lambda d: ar_wait(d + 1))
-    red[...] = jnp.sum(ar[...], axis=0)
-
-    def spread(i):
-        return 4 + (i + 1) // 2 * (2 * (i % 2) - 1)
-
-    def fin_copy(d):
-        return remote(
-            red, fin.at[z], fin_send.at[d], fin_recv.at[z], ((z + d) % 8) * 4 + low, t
-        )
-
-    def fin_wait(d):
-        src = (z + d) % 8
-        remote(red, fin.at[src], fin_send.at[d], fin_recv.at[src], c, t).wait_recv()
-
-    loop(7, lambda i: fin_copy(spread(i)).start())
-    fin[z] = red[...]
-    loop(7, lambda d: fin_wait(d + 1))
-
-    whole = fin[...]
-    sq[...] = jnp.sum(whole * whole, axis=0)
-
-    def sq_copy(d):
-        return remote(sq, sqr.at[t], sq_send.at[d], sq_recv.at[t], c, (t + d) % 8)
-
-    def sq_wait(d):
-        src = (t + d) % 8
-        remote(sq, sqr.at[src], sq_send.at[d], sq_recv.at[src], c, t).wait_recv()
-
-    loop(7, lambda d: sq_copy(d + 1).start())
-    sqr[t] = sq[...]
-    loop(7, lambda d: sq_wait(d + 1))
-    squared = jnp.sum(jnp.sum(jnp.sum(sqr[...], axis=0), axis=0, keepdims=True), axis=1, keepdims=True)
-    factor = jnp.sqrt(
-        float(RANK * (QUERY_HEADS + 2 * KEY_VALUE_HEADS) * HEAD_SIZE) / (squared + 1e-06)
-    )
-    out_ref[...] = fin[...] * factor
-
-    for k in range(9, 11):
+    for k in range(7, 11):
         for n in range(2):
             message(k, n).wait_send()
     for n in range(4):
@@ -511,8 +484,45 @@
     for m in range(4):
         x_part(m).wait_send()
     loop(NRC - 1, lambda rc: x_copy(rc).wait_send())
+    loop(CTX - 1, lambda d: ar_wait(d + 1))
+    red[...] = jnp.sum(ar[...], axis=0)
+
+    def spread(i):
+        return 4 + (i + 1) // 2 * (2 * (i % 2) - 1)
+
+    def fin_copy(d):
+        return remote(
+            red, fin.at[z], fin_send.at[d], fin_recv.at[z], ((z + d) % 8) * 4 + low, t
+        )
+
+    def fin_wait(d):
+        src = (z + d) % 8
+        remote(red, fin.at[src], fin_send.at[d], fin_recv.at[src], c, t).wait_recv()
+
+    loop(7, lambda i: fin_copy(spread(i)).start())
+    fin[z] = red[...]
     loop(CTX - 1, lambda d: ar_copy(d + 1).wait_send())
+    loop(7, lambda d: fin_wait(d + 1))
+
+    whole = fin[...]
+    sq[...] = jnp.sum(whole * whole, axis=0)
+
+    def sq_copy(d):
+        return remote(sq, sqr.at[t], sq_send.at[d], sq_recv.at[t], c, (t + d) % 8)
+
+    def sq_wait(d):
+        src = (t + d) % 8
+        remote(sq, sqr.at[src], sq_send.at[d], sq_recv.at[src], c, t).wait_recv()
+
+    loop(7, lambda d: sq_copy(d + 1).start())
+    sqr[t] = sq[...]
     loop(7, lambda d: fin_copy(d + 1).wait_send())
+    loop(7, lambda d: sq_wait(d + 1))
+    squared = jnp.sum(jnp.sum(jnp.sum(sqr[...], axis=0), axis=0, keepdims=True), axis=1, keepdims=True)
+    factor = jnp.sqrt(
+        float(RANK * (QUERY_HEADS + 2 * KEY_VALUE_HEADS) * HEAD_SIZE) / (squared + 1e-06)
+    )
+    out_ref[...] = fin[...] * factor
     loop(7, lambda d: sq_copy(d + 1).wait_send())
 
 

time: 70.9 us -> 68.4 us (0.965)
  Pallas kernels: 69.7 us -> 67.2 us
    pallas_call x1, Pallas kernels: 68.3 us -> 65.8 us  [per_device(): pl.pallas_call(kernel, out_shape=jax.ShapeDtypeStruct((8, RANK, HEAD_SIZE...]
where the time goes in v5:
time: 68.4 us; the launch traced here: 67.8 us
  Pallas kernels  67.2 us (98%)
    pallas_call x1, Pallas kernels, per_device(): pl.pallas_call(kernel, out_shape=jax.ShapeDtypeStruct((8, RANK, HEAD_SIZE...  65.8 us
    pallas_call x1, Pallas kernels, per_device(): pl.pallas_call(split, out_shape=(jax.ShapeDtypeStruct((RANK, QCOLS), F32)...  1.37 us

profile of v5, /device:TPU:8, one launch (start us, length us, event | category | flops | bytes accessed | tf_op | source)
XLA Modules:
  0.0 67.8 jit_solution(4693656657461604162)
XLA Ops:
  0.6 65.8 %shard_map.112.sum_ref = f32[8,8,128]{2,1,0:T(8,128)} custom-call(bf16[672,512]{1,0:T(8,128)(2,1)} %bitcast.6, bf16[672]{0:T(1024)(128)(2,1)} %nw_ref.1, s32[1,512]{1,0:T(1,128)} %bitcast.9, bf16[512,512]{1,0:T(8,128)(2,1)} %q_ref.1, bf16[512,256]{1,0:T(8,128)(2,1)} %k_ref.1, bf16[512,256]{1,0:T(8,128)(2,1)} %v_ref.1, bf16[672,4096]{1,0:T(8,128)(2,1)} %bitcast.5, ...), custom_call_target="tpu_custom_call" | custom-call | flops 8000000000 | bytes 10000000 | tf_op jit(solution)/shard_map/pallas_call | solution.py:541
  66.5 1.4 %shard_map.113 = (f32[8,512]{1,0:T(8,128)}, f32[8,256]{1,0:T(8,128)}, f32[8,256]{1,0:T(8,128)}) custom-call(f32[8,8,128]{2,1,0:T(8,128)} %shard_map.112.sum_ref), custom_call_target="tpu_custom_call" | custom-call | tf_op jit(solution)/shard_map/pallas_call | solution.py:601

commit v6 on v5

--- a/solution.py
+++ b/solution.py
@@ -404,12 +404,9 @@
     ssend[0] = far[:, 0:256].astype(BF16)
     ssend[1] = far[:, 256:512].astype(BF16)
     issue(5)
-    kv_copy(1, 0).wait_recv()
-    kv_copy(1, 1).start()
-    kv_copy(0, 1).wait_recv()
-    loop(2, softmax)
     pass_on(1)
     issue(6)
+    issue(7)
 
     loop(3, lambda d: t3_wait(d + 1))
     t4s = [
@@ -422,13 +419,18 @@
     for copy in t4s:
         copy.start()
 
+    kv_copy(1, 0).wait_recv()
+    kv_copy(1, 1).start()
+    kv_copy(0, 1).wait_recv()
+    loop(2, softmax)
+
     pl.semaphore_wait(known.at[1], 2)
     meet(known.at[2], 8)
     loop(2, lambda i: softmax(i + 2))
-    issue(7)
-    loop(2, lambda i: softmax(i + 4))
     pass_on(2)
     issue(8)
+    loop(2, lambda i: softmax(i + 4))
+    issue(9)
     finish(0)
     loop(2, lambda i: softmax(i + 6))
 
@@ -444,7 +446,6 @@
         fsend[n, :, passed] = (zbuf[1 + n, :, passed] + srecv[n].astype(F32)).astype(BF16)
         fsend[n, :, direct] = zbuf[1 + n, :, direct].astype(BF16)
 
-    issue(9)
     issue(10)
     for copy in t4s:
         copy.wait()

time: 68.4 us -> 68.4 us (level)
  no operation moved by 1% of the time
where the time goes in v6:
time: 68.4 us; the launch traced here: 67.5 us
  Pallas kernels  66.8 us (98%)
    pallas_call x1, Pallas kernels, per_device(): pl.pallas_call(kernel, out_shape=jax.ShapeDtypeStruct((8, RANK, HEAD_SIZE...  65.5 us
    pallas_call x1, Pallas kernels, per_device(): pl.pallas_call(split, out_shape=(jax.ShapeDtypeStruct((RANK, QCOLS), F32)...  1.37 us

profile of v6, /device:TPU:8, one launch (start us, length us, event | category | flops | bytes accessed | tf_op | source)
XLA Modules:
  0.0 67.5 jit_solution(3180722116838005972)
XLA Ops:
  0.6 65.5 %shard_map.112.sum_ref = f32[8,8,128]{2,1,0:T(8,128)} custom-call(bf16[672,512]{1,0:T(8,128)(2,1)} %bitcast.6, bf16[672]{0:T(1024)(128)(2,1)} %nw_ref.1, s32[1,512]{1,0:T(1,128)} %bitcast.9, bf16[512,512]{1,0:T(8,128)(2,1)} %q_ref.1, bf16[512,256]{1,0:T(8,128)(2,1)} %k_ref.1, bf16[512,256]{1,0:T(8,128)(2,1)} %v_ref.1, bf16[672,4096]{1,0:T(8,128)(2,1)} %bitcast.5, ...), custom_call_target="tpu_custom_call" | custom-call | flops 8000000000 | bytes 10000000 | tf_op jit(solution)/shard_map/pallas_call | solution.py:542
  66.1 1.4 %shard_map.113 = (f32[8,512]{1,0:T(8,128)}, f32[8,256]{1,0:T(8,128)}, f32[8,256]{1,0:T(8,128)}) custom-call(f32[8,8,128]{2,1,0:T(8,128)} %shard_map.112.sum_ref), custom_call_target="tpu_custom_call" | custom-call | tf_op jit(solution)/shard_map/pallas_call | solution.py:602
